TPU v7x, 32 devices: a whole 2x2x4 slice. The times are simulated.
32 devices in a mesh: cand: 2 (over x), tp: 4 (over z), dp: 4 (over y, core).
Axes of the slice: x: 2, y: 2, z: 4, core: 2. Of those that a mesh axis runs over, the one named last changes fastest.
Arguments:
- tokens: bfloat16 [4, 4, 256, 4096], P('dp', 'cand')
- qkv_weight: bfloat16 [4096, 4, 768], P(None, 'tp'), may hold values from -0.09375 to 0.09375
- lengths: int32 [4, 4], P('dp', 'cand'), may hold values from 64 to 256, as said below
- grad_out: bfloat16 [4, 4, 256, 4, 512], P('dp', 'cand', None, 'tp')
Outputs:
- attended: bfloat16 [4, 4, 256, 4, 512], P('dp', 'cand', None, 'tp')
- grad_x: bfloat16 [4, 4, 256, 4096], P('dp', 'cand', None, 'tp')
- grad_w: float32 [4096, 4, 768], P(('cand', 'dp'), 'tp')
Inputs may be any that keep to these rules, and one draw needn't show every extreme that they name: `lengths`: some passage in each draw has all 256 tokens in use.
All inputs are finite; a program needn't handle non-finite values.
Results may differ from a plain program's by a relative error of at most 0.006.
The roundings to bfloat16 on the way count: a program that leaves them out, or rounds other values in their place, can miss the bound.
Values may be sent and summed in bfloat16 or wider, within the bound.
A program may use at most 128 MiB of HBM per device.

v0:
```python
import math

import jax
import jax.numpy as jnp
from jax import lax
from jax.sharding import PartitionSpec as P

GQ = 4
HD = 128


highest = lax.Precision.HIGHEST
masked_value = -1e30


def attend(queries, key_rows, value_rows, cls_keys, cls_values, lengths, first_index):
    head_size = queries.shape[-1]
    factor = 1.0 / math.sqrt(head_size)
    cand_total = queries.shape[0]
    seq_len = queries.shape[1]
    listed = cls_keys.shape[0]
    scores = jnp.einsum("clhge,cmhe->chglm", queries, key_rows, precision=highest) * factor
    visible = jnp.arange(seq_len)[None, :] < lengths[:, None]
    scores = jnp.where(visible[:, None, None, None, :], scores, masked_value)
    row_peak = lax.stop_gradient(jnp.max(scores, axis=-1, keepdims=True))
    weights = jnp.exp(scores - row_peak)
    totals = jnp.sum(weights, axis=-1)
    blended = jnp.einsum("chglm,cmhe->clhge", weights, value_rows, precision=highest)
    blended = blended / jnp.transpose(totals, (0, 3, 1, 2))[..., None]
    across = jnp.einsum("chge,ahe->chga", queries[:, 0], cls_keys, precision=highest) * factor
    own_slot = jnp.arange(listed)[None, :] == (first_index + jnp.arange(cand_total))[:, None]
    across = jnp.where(own_slot[:, None, None, :], masked_value, across)
    first_row = scores[:, :, :, 0, :]
    joint_peak = lax.stop_gradient(
        jnp.maximum(jnp.max(first_row, axis=-1), jnp.max(across, axis=-1))
    )[..., None]
    local_weights = jnp.exp(first_row - joint_peak)
    far_weights = jnp.exp(across - joint_peak)
    denominator = jnp.sum(local_weights, axis=-1) + jnp.sum(far_weights, axis=-1)
    head_row = jnp.einsum("chgm,cmhe->chge", local_weights, value_rows, precision=highest)
    head_row = head_row + jnp.einsum("chga,ahe->chge", far_weights, cls_values, precision=highest)
    head_row = head_row / denominator[..., None]
    return blended.at[:, 0].set(head_row)


def body(tokens, qkv_weight, lengths, grad_out):
    list_count, cand_count, seq_len, model_width = tokens.shape
    local_heads = qkv_weight.shape[1]
    row_count = list_count * cand_count * seq_len
    flat_rows = tokens.reshape(row_count, model_width)
    weight_mat = qkv_weight.reshape(model_width, -1)
    packed = jnp.dot(flat_rows, weight_mat, preferred_element_type=jnp.float32).astype(jnp.bfloat16)
    packed = packed.reshape(list_count, cand_count, seq_len, local_heads, (GQ + 2) * HD)
    query_part = packed[..., : GQ * HD].reshape(
        list_count, cand_count, seq_len, local_heads, GQ, HD
    )
    key_part = packed[..., GQ * HD : (GQ + 1) * HD]
    value_part = packed[..., (GQ + 1) * HD :]
    cls_keys, cls_values = (
        lax.all_gather(key_part[:, :, 0], "cand", axis=1, tiled=True),
        lax.all_gather(value_part[:, :, 0], "cand", axis=1, tiled=True),
    )
    first_index = lax.axis_index("cand") * cand_count

    def forward(q_in, k_in, v_in, ck_in, cv_in):
        return jax.vmap(attend, in_axes=(0, 0, 0, 0, 0, 0, None))(
            q_in, k_in, v_in, ck_in, cv_in, lengths, first_index
        )

    result, pullback = jax.vjp(
        forward,
        query_part.astype(jnp.float32),
        key_part.astype(jnp.float32),
        value_part.astype(jnp.float32),
        cls_keys.astype(jnp.float32),
        cls_values.astype(jnp.float32),
    )
    attended = result.reshape(list_count, cand_count, seq_len, local_heads, GQ * HD).astype(
        jnp.bfloat16
    )
    upstream = grad_out.astype(jnp.float32).reshape(
        list_count, cand_count, seq_len, local_heads, GQ, HD
    )
    d_query, d_key, d_value, d_cls_key, d_cls_value = pullback(upstream)
    own_key, own_value = (
        lax.psum_scatter(d_cls_key, "cand", scatter_dimension=1, tiled=True),
        lax.psum_scatter(d_cls_value, "cand", scatter_dimension=1, tiled=True),
    )
    d_key = d_key.at[:, :, 0].add(own_key)
    d_value = d_value.at[:, :, 0].add(own_value)
    d_packed = jnp.concatenate(
        [d_query.reshape(list_count, cand_count, seq_len, local_heads, GQ * HD), d_key, d_value],
        axis=-1,
    )
    d_packed = d_packed.astype(jnp.bfloat16).reshape(row_count, -1)
    partial_x = lax.dot_general(
        d_packed, weight_mat, (((1,), (1,)), ((), ())), preferred_element_type=jnp.float32
    )
    grad_x = lax.psum_scatter(partial_x, "tp", scatter_dimension=1, tiled=True).astype(jnp.bfloat16)
    grad_x = grad_x.reshape(list_count, cand_count, seq_len, -1)
    grad_w = lax.psum_scatter(
        lax.dot_general(
            flat_rows, d_packed, (((0,), (0,)), ((), ())), preferred_element_type=jnp.float32
        ),
        ("cand", "dp"),
        scatter_dimension=0,
        tiled=True,
    )
    return (attended, grad_x, grad_w.reshape(grad_w.shape[0], local_heads, -1))


def solution(mesh):
    placed = (
        P("dp", "cand", None, None),
        P(None, "tp", None),
        P("dp", "cand"),
        P("dp", "cand", None, "tp", None),
    )
    return jax.shard_map(
        body,
        mesh=mesh,
        in_specs=placed,
        out_specs=(
            P("dp", "cand", None, "tp", None),
            P("dp", "cand", None, "tp"),
            P(("cand", "dp"), "tp", None),
        ),
        check_vma=False,
    )
```

profile of v0, /device:TPU:0, one launch (start us, length us, event | category | flops | bytes accessed | tf_op | source)
XLA Modules:
  0.0 340.1 jit_solution(12469537433071320357)
XLA Ops:
  7.2 7.5 %fusion.14 = bf16[512,768]{1,0:T(8,128)(2,1)S(1)} fusion(bf16[512,4096]{1,0:T(8,128)(2,1)} %bitcast.241, bf16[4096,1,768]{2,0,1:T(8,128)(2,1)} %param.13), kind=kOutput, calls=%fused_computation.19 | convolution fusion | flops 3221618688 | bytes 11272192 | tf_op jit(solution)/shard_map/dot_general | solution.py:52
  16.9 5.1 %all-gather = bf16[1,4,1,1,128]{4,3,2,0,1:T(2,128)(2,1)S(1)} all-gather(bf16[1,2,1,1,128]{4,3,2,0,1:T(2,128)(2,1)S(1)} %get-tuple-element.77), channel_id=2, replica_groups=mesh['cand'=2,'tp'=4,'dp'=4] {'cand'}, dimensions={1}, use_global_device_ids=true | all-gather | bytes 1536 | tf_op jit(solution)/shard_map/all_gather | solution.py:60
  23.2 1.2 copy.128
  24.8 4.4 %all-gather.1 = bf16[1,4,1,1,128]{4,3,2,0,1:T(2,128)(2,1)S(1)} all-gather(bf16[1,2,1,1,128]{4,3,2,0,1:T(2,128)(2,1)S(1)} %get-tuple-element.76), channel_id=3, replica_groups=mesh['cand'=2,'tp'=4,'dp'=4] {'cand'}, dimensions={1}, use_global_device_ids=true | all-gather | bytes 1536 | tf_op jit(solution)/shard_map/all_gather | solution.py:61
  29.3 1.2 fusion.48
  30.6 1.2 fusion.25
  32.1 4.5 %fusion.32 = (f32[2,4,256]{1,0,2:T(2,128)}, f32[2,4,256,256]{3,1,0,2:T(4,128)}) fusion(f32[2,4,256]{1,0,2:T(2,128)S(1)} %copy.117, f32[1,2,1,4,256,256]{5,4,3,1,2,0:T(8,128)S(1)} %get-tuple-element.79), kind=kLoop, calls=%fused_computation.47 | loop fusion | flops 1046528 | bytes 4210688 | tf_op jit(solution)/shard_map/jvp(vmap())/reduce_sum | solution.py:27
  36.7 1.1 copy.121
  37.8 4.6 %broadcast_divide_fusion.1 = (bf16[1,2,256,1,4,128]{2,5,4,1,3,0:T(8,128)(2,1)}, f32[1,2,256,1,4,128]{2,5,4,1,3,0:T(8,128)}) fusion(f32[2,256,4]{1,2,0:T(4,128)S(1)} %bitcast.263, f32[2,4,256,256]{3,1,0,2:T(4,128)} %get-tuple-element.73, bf16[1,2,256,1,768]{4,2,1,3,0:T(8,128)(2,1)} %bitcast.255), kind=kOutput, calls=%fused_computation.46 | convolution fusion | flops 805830656 | bytes 3809280 | tf_op jit(solution)/shard_map/jvp(vmap(chglm,cmhe->clhge))/dot_general | solution.py:28
  43.2 1.4 scatter.9
  44.6 3.3 fusion.29
  49.0 7.4 %fusion.7 = f32[2,256,256,4]{1,3,0,2:T(4,128)} fusion(f32[2,4,256,256]{3,2,1,0:T(8,128)} %fusion.29, f32[1,2,1,4,1,256]{5,3,1,4,2,0:T(4,128)S(1)} %fusion.25, f32[2,4,256]{1,0,2:T(2,128)} %copy.132, pred[2,256]{1,0:T(4,128)(4,1)S(1)} %iota_compare_fusion.1, f32[2,4,256]{1,0,2:T(2,128)S(1)} %copy.117, f32[1,2,1,4,256,256]{5,4,3,1,2,0:T(8,128)S(1)} %get-tuple-element.79), kind=kLoop, calls=%fused_computation.9 | loop fusion | flops 3145728 | bytes 6316544 | tf_op jit(solution)/shard_map/reshape.222
  56.4 2.2 copy.137
  58.6 3.7 %fusion.38 = f32[2,256,4,128]{3,1,2,0:T(8,128)} fusion(f32[2,256,256,4]{2,1,3,0:T(8,128)S(1)} %copy.137, bf16[1,2,256,1,768]{4,2,1,3,0:T(8,128)(2,1)} %bitcast.257), kind=kOutput, calls=%fused_computation.55 | convolution fusion | flops 805306368 | bytes 3276800 | tf_op jit(solution)/shard_map/transpose(jvp(vmap(clhge,cmhe->chglm)))/dot_general | solution.py:22
  62.4 1.1 fusion.72
  64.8 3.6 %fusion.20 = f32[2,128,256]{2,1,0:T(8,128)S(1)} fusion(f32[2,4,256,256]{3,1,0,2:T(4,128)} %get-tuple-element.73, f32[1,2,256,1,4,128]{2,5,4,1,3,0:T(8,128)S(1)} %scatter.9, f32[2,256,4]{1,2,0:T(4,128)S(1)} %bitcast.265), kind=kOutput, calls=%fused_computation.21 | convolution fusion | flops 805568512 | bytes 3416064 | tf_op jit(solution)/shard_map/transpose(jvp(vmap(chglm,cmhe->clhge)))/dot_general | solution.py:28
  69.6 4.9 %all-reduce.4 = (f32[1,4,1,128]{3,1,2,0:T(4,128)S(1)}, f32[1,4,1,128]{3,1,2,0:T(4,128)S(1)}) all-reduce(f32[1,4,1,128]{3,1,2,0:T(4,128)S(1)} %convolution_bitcast_fusion.4, f32[1,4,1,128]{3,1,2,0:T(4,128)S(1)} %convolution_bitcast_fusion.5), channel_id=5, replica_groups=mesh['cand'=2,'tp'=4,'dp'=4] {'cand'}, use_global_device_ids=true, to_apply=%region_9.10.clone | all-reduce | flops 1024 | bytes 8192
  77.0 8.4 %fusion = f32[512,4096]{1,0:T(8,128)} fusion(bf16[4096,1,768]{2,0,1:T(8,128)(2,1)} %param.13, bf16[512,128]{1,0:T(8,128)(2,1)S(1)} %bitcast.260, bf16[512,128]{1,0:T(8,128)(2,1)S(1)} %bitcast.258, bf16[512,512]{1,0:T(8,128)(2,1)S(1)} %bitcast.243), kind=kOutput, calls=%fused_computation.1 | convolution fusion | flops 3223584768 | bytes 15466496 | tf_op jit(solution)/shard_map/dot_general | solution.py:96
  85.4 8.9 %convolution_bitcast_fusion = f32[4096,768]{0,1:T(8,128)} fusion(bf16[512,4096]{1,0:T(8,128)(2,1)} %bitcast.242, bf16[512,128]{1,0:T(8,128)(2,1)S(1)} %bitcast.261, bf16[512,128]{1,0:T(8,128)(2,1)S(1)} %bitcast.259, bf16[512,512]{1,0:T(8,128)(2,1)S(1)} %bitcast.244), kind=kOutput, calls=%fused_computation | convolution fusion | flops 3223584768 | bytes 17563648 | tf_op jit(solution)/shard_map/dot_general | solution.py:102
  95.9 1.0 copy.145
  96.9 134.9 %reduce-scatter.5.cloned.1.call-done = f32[512,1024]{1,0:T(8,128)} async-done(((f32[512,4096]{1,0:T(8,128)}), f32[512,1024]{1,0:T(8,128)}) %reduce-scatter.5.cloned.1.call-update) | async-done | bytes 2097168 | tf_op jit(solution)/shard_map/reduce_scatter | solution.py:99
  231.8 2.7 convert_element_type.33
  234.5 93.9 %reduce-scatter.7.cloned.1.call-done = f32[512,768]{0,1:T(8,128)} async-done(((f32[4096,768]{0,1:T(8,128)}), f32[512,768]{0,1:T(8,128)}) %reduce-scatter.7.cloned.1.call-update) | async-done | bytes 1572880 | tf_op jit(solution)/shard_map/reduce_scatter | solution.py:101
  328.5 4.8 %copy.146 = f32[512,1,768]{2,1,0:T(1,128)} copy(f32[512,1,768]{0,2,1:T(8,128)} %bitcast.246) | data formatting | bytes 3145728
  (70 shorter events, 12.0 us)
Async XLA Ops:
  7.2 224.7 %reduce-scatter.5.cloned.1.call-start = ((), (), s32[]{:S(2)}) async-start(), calls=%async_computation.2 | async-start | bytes 10485760 | tf_op jit(solution)/shard_map/reduce_scatter | solution.py:99
  14.7 2.1 copy-start.4
  14.7 1.3 copy-start.6
  15.0 8.1 %copy-start = (bf16[1,2,256,1,512]{2,4,1,3,0:T(8,128)(2,1)}, bf16[1,2,256,1,512]{2,4,1,3,0:T(8,128)(2,1)S(1)}, u32[]{:S(2)}) copy-start(bf16[1,2,256,1,512]{2,4,1,3,0:T(8,128)(2,1)S(1)} %copy.115) | copy-start | bytes 1572868
  44.6 3.3 copy-start.3
  58.6 3.8 %copy-start.1 = (bf16[1,2,256,1,512]{2,4,1,3,0:T(8,128)(2,1)S(1)}, bf16[1,2,256,1,512]{2,4,1,3,0:T(8,128)(2,1)}, u32[]{:S(2)}) copy-start(bf16[1,2,256,1,512]{2,4,1,3,0:T(8,128)(2,1)} %copy-done) | copy-start | bytes 1572868
  64.8 3.6 %copy-start.2 = (f32[2,256,4,128]{3,1,2,0:T(8,128)S(1)}, f32[2,256,4,128]{3,1,2,0:T(8,128)}, u32[]{:S(2)}) copy-start(f32[2,256,4,128]{3,1,2,0:T(8,128)} %fusion.38) | copy-start | bytes 3145732
  68.4 6.1 %copy-start.7 = (u32[32]{0:T(128)S(1)}, u32[32]{0:T(128)}, u32[]{:S(2)}) copy-start(u32[32]{0:T(128)} %constant.132) | copy-start | bytes 388
  85.4 243.1 %reduce-scatter.7.cloned.1.call-start = ((), (), s32[]{:S(2)}) async-start(), calls=%async_computation.3 | async-start | bytes 14155776 | tf_op jit(solution)/shard_map/reduce_scatter | solution.py:101
  94.3 1.0 copy-start.5
Sparse Core Ops, SparseCore 0:
  85.5 146.2 reduce-scatter.4
  235.3 93.1 reduce-scatter.6
where the time goes:
time: 341 us; the launch traced here: 340 us
  waiting for transfers between devices  229 us (67%)
  matrix products  47.1 us (14%)
  local copies, waits for them, and re-layouts  18.3 us (5%)
  other arithmetic  16.4 us (5%)
  between operations  15 us (4%)
  blocking collectives  14.5 us (4%)
    reduce_scatter x1, waiting for transfers between devices, body(): lax.psum_scatter(partial_x, 'tp', scatter_dimension=1, tiled=True)  135 us
    reduce_scatter x1, waiting for transfers between devices, body(): lax.psum_scatter(lax.dot_general(flat_rows, d_packed, (((0,), (0,)), ((),...  93.9 us
    dot_general x3, matrix products, attend(): jnp.einsum('chglm,cmhe->clhge', weights, value_rows, precision=highest)  11.5 us
    dot_general x1, matrix products, body(): lax.dot_general(flat_rows, d_packed, (((0,), (0,)), ((), ())), preferred_...  8.86 us
    dot_general x1, matrix products, body(): lax.dot_general(d_packed, weight_mat, (((1,), (1,)), ((), ())), preferred...  8.39 us
    another operation x6, other arithmetic  8.3 us
    dot_general x1, matrix products, body(): jnp.dot(flat_rows, weight_mat, preferred_element_type=jnp.float32)  7.47 us
    unnamed x20, local copies, waits for them, and re-layouts  7.25 us
  transfers between devices with their start and end apart: 2, of which 2 were waited for; matrix products, arithmetic and copies ran while one was open for 4% of the time, Pallas kernels for 0%

commit v1 on v0

--- a/solution.py
+++ b/solution.py
@@ -1,8 +1,11 @@
+import functools
 import math
 
 import jax
 import jax.numpy as jnp
 from jax import lax
+from jax.experimental import pallas as pl
+from jax.experimental.pallas import tpu as pltpu
 from jax.sharding import PartitionSpec as P
 
 GQ = 4
@@ -109,6 +112,502 @@
     return (attended, grad_x, grad_w.reshape(grad_w.shape[0], local_heads, -1))
 
 
+MESH = pl.DeviceIdType.MESH
+f32 = jnp.float32
+bf16 = jnp.bfloat16
+
+
+def dot(a, b, ca, cb):
+    return lax.dot_general(a, b, (((ca,), (cb,)), ((), ())), preferred_element_type=f32)
+
+
+def split(x):
+    hi = x.astype(bf16)
+    return hi, (x - hi.astype(f32)).astype(bf16)
+
+
+def dot2(x, b, ca, cb):
+    return dot(x[0], b, ca, cb) + dot(x[1], b, ca, cb)
+
+
+def kernel(
+    sizes,
+    tok,
+    w,
+    lens,
+    go,
+    att,
+    gx,
+    gw,
+    qb,
+    kvb,
+    cls,
+    dcls,
+    dclsr,
+    dkv_acc,
+    gx_acc,
+    tokg,
+    wg,
+    dqz,
+    dkvz,
+    dqp,
+    dkvp,
+    cls_s,
+    cls_r,
+    dcls_s,
+    dcls_r,
+    tok_s,
+    tok_r,
+    wz_s,
+    wz_r,
+    wp_s,
+    wp_r,
+    wf_s,
+    z_s,
+    z_r,
+    zf_s,
+    p_s,
+    p_r,
+    pf_s,
+):
+    nc, nt, nd, own, length = sizes
+    ne = nc * nd
+    c, t, d = lax.axis_index("cand"), lax.axis_index("tp"), lax.axis_index("dp")
+    e = c * nd + d
+    sib = d + 1 - 2 * lax.rem(d, 2)
+    cols = tok.shape[1] // ne
+    xcols = w.shape[0] // nt
+    part = xcols // ne
+    rows = own * length
+    scale = 1.0 / math.sqrt(HD)
+
+    cls[...] = jnp.zeros_like(cls)
+    dcls[...] = jnp.zeros_like(dcls)
+    dkv_acc[...] = jnp.zeros_like(dkv_acc)
+
+    def plane(k):
+        j = lax.rem(e + k, ne)
+        return j, {"cand": j // nd, "dp": lax.rem(j, nd)}
+
+    nh = nd // 2
+
+    def chip(k):
+        j = lax.rem(c * nh + d // 2 + k, nc * nh)
+        jc, jd = j // nh, 2 * lax.rem(j, nh) + lax.rem(d, 2)
+        return jc * nd + jd, {"cand": jc, "dp": jd}
+
+    barrier = pltpu.get_barrier_semaphore()
+    for k in range(1, ne):
+        pl.semaphore_signal(barrier, inc=1, device_id=plane(k)[1], device_id_type=MESH)
+    for k in range(1, nt):
+        pl.semaphore_signal(
+            barrier, inc=1, device_id={"tp": lax.rem(t + k, nt)}, device_id_type=MESH
+        )
+    pl.semaphore_wait(barrier, ne - 1 + nt - 1)
+
+    def remote(src, dst, ss, rs, dev):
+        return pltpu.make_async_remote_copy(
+            src_ref=src, dst_ref=dst, send_sem=ss, recv_sem=rs, device_id=dev, device_id_type=MESH
+        )
+
+    def wz_send(k):
+        o = lax.rem(t + k, nt)
+        return remote(
+            w.at[pl.ds(pl.multiple_of(o * xcols + e * part, 16), part)],
+            wg.at[t, e],
+            wz_s.at[k],
+            wz_r.at[t],
+            {"tp": o},
+        )
+
+    def wz_recv(k):
+        h = lax.rem(t + k, nt)
+        return remote(wg.at[h, e], wg.at[h, e], wz_s.at[k], wz_r.at[h], {"tp": h})
+
+    def wp_send(k, h):
+        return remote(wg.at[h, e], wg.at[h, e], wp_s.at[k, h], wp_r.at[e, h], chip(k)[1])
+
+    def wp_sib(j, k, h):
+        return remote(wg.at[h, j], wg.at[h, j], wf_s.at[k, h], wp_r.at[j, h], {"dp": sib})
+
+    def w_wait(j, h):
+        remote(wg.at[h, j], wg.at[h, j], wf_s.at[0, h], wp_r.at[j, h], {"dp": sib}).wait_recv()
+
+    def tok_send(k):
+        j, dev = plane(k)
+        return remote(
+            tok.at[:, pl.ds(pl.multiple_of(j * cols, 128), cols)],
+            tokg.at[e],
+            tok_s.at[k],
+            tok_r.at[e],
+            dev,
+        )
+
+    for k in range(1, nt):
+        wz_send(k).start()
+    for k in range(1, ne):
+        tok_send(k).start()
+
+    def zbuf(n, s):
+        return dqz.at[s, n] if n < own else dkvz.at[s]
+
+    def pbuf(n, s):
+        return dqp.at[s, n] if n < own else dkvp.at[s]
+
+    def z_copy(n, s, to, ss):
+        return remote(zbuf(n, s), zbuf(n, s), ss, z_r.at[n, s], {"tp": to})
+
+    def p_send(n, k):
+        return remote(zbuf(n, t), pbuf(n, e), p_s.at[n, k], p_r.at[n, e], chip(k)[1])
+
+    def p_sib(n):
+        return remote(zbuf(n, t), pbuf(n, e), pf_s.at[n, 0], p_r.at[n, e], {"dp": sib})
+
+    def p_fwd(n, j, k):
+        return remote(pbuf(n, j), pbuf(n, j), pf_s.at[n, k], p_r.at[n, j], {"dp": sib})
+
+    def p_wait(n, j):
+        remote(pbuf(n, j), pbuf(n, j), pf_s.at[n, 0], p_r.at[n, j], {"dp": sib}).wait_recv()
+
+    def send_chunk(n):
+        for side in (0, 1):
+            to = t + 2 * side - 1
+
+            @pl.when((to >= 0) & (to < nt))
+            def _():
+                z_copy(n, t, to, z_s.at[n, side]).start()
+
+        for k in range(1, nc * nh):
+            p_send(n, k).start()
+        p_sib(n).start()
+
+    kvb[...] = dot(tok[...], w[:, GQ * HD :], 1, 0).astype(bf16)
+    first = lax.broadcasted_iota(jnp.int32, (16, 2 * HD), 0)
+    mine = jnp.zeros((16, 2 * HD), f32)
+    for p in range(own):
+        row = kvb[p * length : p * length + 16, :].astype(f32)[0:1]
+        mine = jnp.where(first == p, row, mine)
+    c16 = pl.ds(pl.multiple_of(c * 16, 16), 16)
+    cls[c16, :] = mine.astype(bf16)
+
+    def cls_send(k):
+        return remote(
+            cls.at[c16], cls.at[c16], cls_s.at[k], cls_r.at[c], {"cand": lax.rem(c + k, nc)}
+        )
+
+    def cls_recv(k):
+        o = lax.rem(c + k, nc)
+        o16 = pl.ds(pl.multiple_of(o * 16, 16), 16)
+        return remote(cls.at[o16], cls.at[o16], cls_s.at[k], cls_r.at[o], {"cand": o})
+
+    for k in range(1, nc):
+        cls_send(k).start()
+
+    @pl.loop(0, GQ * HD // 256)
+    def _(i):
+        at = pl.ds(pl.multiple_of(i * 256, 256), 256)
+        qb[:, at] = dot(tok[...], w[:, at], 1, 0).astype(bf16)
+
+    for k in range(1, nc):
+        cls_recv(k).wait_recv()
+
+    far_lane = lax.broadcasted_iota(jnp.int32, (16, 128), 1)
+    far_row = lax.broadcasted_iota(jnp.int32, (16, 128), 0)
+    lane = lax.broadcasted_iota(jnp.int32, (length, length), 1)
+
+    for p in range(own):
+        at = slice(p * length, (p + 1) * length)
+        visible = lane < lens[p]
+        listed = (far_row == 0) & (lax.rem(far_lane, 16) < own) & (far_lane < nc * 16)
+        listed = listed & (far_lane != c * 16 + p)
+
+        @pl.loop(0, GQ)
+        def _(g):
+            head = pl.ds(pl.multiple_of(g * HD, HD), HD)
+            q, do = qb[at, head], go[at, head]
+            k, v = kvb[at, :HD], kvb[at, HD:]
+            ck, cv = cls[:, :HD], cls[:, HD:]
+            q16, do16 = q[:16], do[:16]
+            s = jnp.where(visible, dot(q, k, 1, 1) * scale, masked_value)
+            f = jnp.where(listed, dot(q16, ck, 1, 1) * scale, masked_value)
+            m = jnp.max(s, axis=1, keepdims=True)
+            m16 = jnp.maximum(m[:16], jnp.max(f, axis=1, keepdims=True))
+            m = jnp.concatenate([m16, m[16:]], axis=0)
+            pr, pf = jnp.exp(s - m), jnp.exp(f - m16)
+            total = jnp.sum(pr, axis=1, keepdims=True)
+            t16 = total[:16] + jnp.sum(pf, axis=1, keepdims=True)
+            total = jnp.concatenate([t16, total[16:]], axis=0)
+            pr, pf = pr / total, pf / t16
+            prs, pfs = split(pr), split(pf)
+            o = dot2(prs, v, 1, 0)
+            o = jnp.concatenate([o[:16] + dot2(pfs, cv, 1, 0), o[16:]], axis=0)
+            att[at, head] = o.astype(bf16)
+            delta = jnp.sum(o * do.astype(f32), axis=1, keepdims=True)
+            ds = split(pr * (dot(do, v, 1, 1) - delta) * scale)
+            dsf = split(pf * (dot(do16, cv, 1, 1) - delta[:16]) * scale)
+            dq = dot2(ds, k, 1, 0)
+            dq = jnp.concatenate([dq[:16] + dot2(dsf, ck, 1, 0), dq[16:]], axis=0)
+            dqz[t, p, :, head] = dq.astype(bf16)
+            dkv_acc[at, :HD] += dot2(ds, q, 0, 0)
+            dkv_acc[at, HD:] += dot2(prs, do, 0, 0)
+            dcls[:, :HD] += dot2(dsf, q16, 0, 0)
+            dcls[:, HD:] += dot2(pfs, do16, 0, 0)
+
+        if p == own - 1:
+            def dcls_send(k):
+                o = lax.rem(c + k, nc)
+                o16 = pl.ds(pl.multiple_of(o * 16, 16), 16)
+                return remote(dcls.at[o16], dclsr.at[c], dcls_s.at[k], dcls_r.at[c], {"cand": o})
+
+            for k in range(1, nc):
+                dcls_send(k).start()
+        send_chunk(p)
+        if p == 0:
+            for k in range(1, nt):
+                wz_recv(k).wait_recv()
+            for k in range(1, nt):
+                h = lax.rem(t + k, nt)
+                for j in range(1, nc * nh):
+                    wp_send(j, h).start()
+                wp_sib(e, 0, h).start()
+
+    mine = dcls[c16, :]
+    for k in range(1, nc):
+        o = lax.rem(c + k, nc)
+        remote(dclsr.at[o], dclsr.at[o], dcls_s.at[k], dcls_r.at[o], {"cand": o}).wait_recv()
+        mine = mine + dclsr[o]
+    top = lax.broadcasted_iota(jnp.int32, (8, 2 * HD), 0)
+    for p in range(own):
+        at = slice(p * length, p * length + 8)
+        dkv_acc[at, :] = dkv_acc[at, :] + jnp.where(top == 0, mine[p : p + 1], 0.0)
+    dkvz[t] = dkv_acc[...].astype(bf16)
+    send_chunk(own)
+
+    def x_terms(h, weight, start):
+        @pl.loop(0, xcols // part)
+        def _(i):
+            wi = weight(i)
+            at = pl.ds(pl.multiple_of(i * part, 128), part)
+            for p in range(own):
+                rs = slice(p * length, (p + 1) * length)
+                y = dot(dqz[h, p], wi[:, : GQ * HD], 1, 1)
+                y = y + dot(dkvz[h, rs, :], wi[:, GQ * HD :], 1, 1)
+                if start:
+                    gx_acc[rs, at] = y
+                else:
+                    gx_acc[rs, at] += y
+
+    def w_terms(x, dq, dkv, start):
+        xs = [x[p * length : (p + 1) * length] for p in range(own)]
+        y = dot(xs[0], dq(0), 0, 0)
+        for p in range(1, own):
+            y = y + dot(xs[p], dq(p), 0, 0)
+        z = dot(x, dkv, 0, 0)
+        if start:
+            gw[:, : GQ * HD] = y
+            gw[:, GQ * HD :] = z
+        else:
+            gw[:, : GQ * HD] += y
+            gw[:, GQ * HD :] += z
+
+    x_terms(
+        t, lambda i: w[pl.ds(pl.multiple_of(t * xcols + i * part, 16), part), :], True
+    )
+    w_terms(
+        tok[:, pl.ds(pl.multiple_of(e * cols, 128), cols)],
+        lambda p: dqz[t, p],
+        dkvz[t],
+        True,
+    )
+
+    for n in range(own + 1):
+        for k in range(1, nc * nh):
+            j = chip(k)[0]
+            p_wait(n, j)
+            p_fwd(n, j, k).start()
+        for side in (0, 1):
+            src, to = t + 2 * side - 1, t - 2 * side + 1
+
+            @pl.when((src >= 0) & (src < nt))
+            def _():
+                z_copy(n, src, t, zf_s.at[n, 1, side]).wait_recv()
+
+                @pl.when((to >= 0) & (to < nt))
+                def _():
+                    z_copy(n, src, to, zf_s.at[n, 1, side]).start()
+
+    for k in range(1, nc * nh):
+        j = chip(k)[0]
+        for i in range(1, nt):
+            h = lax.rem(t + i, nt)
+            w_wait(j, h)
+            wp_sib(j, k, h).start()
+
+    for dist in range(2, nt):
+        for n in range(own + 1):
+            for side in (0, 1):
+                src, to = t + dist * (2 * side - 1), t - 2 * side + 1
+
+                @pl.when((src >= 0) & (src < nt))
+                def _():
+                    z_copy(n, src, t, zf_s.at[n, dist, side]).wait_recv()
+                    if dist < nt - 1:
+
+                        @pl.when((to >= 0) & (to < nt))
+                        def _():
+                            z_copy(n, src, to, zf_s.at[n, dist, side]).start()
+
+    for k in range(nc * nh):
+        j = chip(k)[0]
+        js = j + 1 - 2 * lax.rem(d, 2)
+        for i in range(1, nt):
+            w_wait(js, lax.rem(t + i, nt))
+
+    @pl.loop(1, nt)
+    def _(i):
+        h = lax.rem(t + i, nt)
+        x_terms(h, lambda i: wg[h, i], False)
+
+    gx[...] = gx_acc[...].astype(bf16)
+
+    for k in range(nc * nh):
+        j = chip(k)[0]
+        js = j + 1 - 2 * lax.rem(d, 2)
+        for n in range(own + 1):
+            p_wait(n, js)
+    for k in range(1, ne):
+        j = plane(k)[0]
+        remote(tokg.at[j], tokg.at[j], tok_s.at[k], tok_r.at[j], {"dp": sib}).wait_recv()
+
+    @pl.loop(1, ne)
+    def _(k):
+        j = lax.rem(e + k, ne)
+        w_terms(tokg[j], lambda p: dqp[j, p], dkvp[j], False)
+
+    for k in range(1, nt):
+        wz_send(k).wait_send()
+    for k in range(1, ne):
+        tok_send(k).wait_send()
+    for k in range(1, nc):
+        cls_send(k).wait_send()
+        o = lax.rem(c + k, nc)
+        o16 = pl.ds(pl.multiple_of(o * 16, 16), 16)
+        remote(dcls.at[o16], dclsr.at[c], dcls_s.at[k], dcls_r.at[c], {"cand": o}).wait_send()
+    for i in range(1, nt):
+        h = lax.rem(t + i, nt)
+        for k in range(1, nc * nh):
+            wp_send(k, h).wait_send()
+            wp_sib(chip(k)[0], k, h).wait_send()
+        wp_sib(e, 0, h).wait_send()
+    for n in range(own + 1):
+        for side in (0, 1):
+            to = t + 2 * side - 1
+
+            @pl.when((to >= 0) & (to < nt))
+            def _():
+                z_copy(n, t, to, z_s.at[n, side]).wait_send()
+
+            for dist in range(1, nt - 1):
+                src, on = t + dist * (2 * side - 1), t - 2 * side + 1
+
+                @pl.when((src >= 0) & (src < nt) & (on >= 0) & (on < nt))
+                def _():
+                    z_copy(n, src, on, zf_s.at[n, dist, side]).wait_send()
+
+        for k in range(1, nc * nh):
+            p_send(n, k).wait_send()
+            p_fwd(n, chip(k)[0], k).wait_send()
+        p_sib(n).wait_send()
+
+
+def fused(sizes, tokens, qkv_weight, lengths, grad_out):
+    nc, nt, nd, own, length = sizes
+    ne, width, rows = nc * nd, tokens.shape[-1], own * length
+    cols, xcols = width // ne, width // nt
+    kv, heads = 2 * HD, GQ * HD
+    dma = pltpu.SemaphoreType.DMA
+    vmem = pl.BlockSpec(memory_space=pltpu.VMEM)
+    flops = 6 * rows * width * (heads + kv)
+    attended, grad_x, grad_w = pl.pallas_call(
+        functools.partial(kernel, sizes),
+        out_shape=(
+            jax.ShapeDtypeStruct((rows, heads), bf16),
+            jax.ShapeDtypeStruct((rows, xcols), bf16),
+            jax.ShapeDtypeStruct((cols, heads + kv), f32),
+        ),
+        in_specs=[vmem, vmem, pl.BlockSpec(memory_space=pltpu.SMEM), vmem],
+        out_specs=(vmem, vmem, vmem),
+        scratch_shapes=[
+            pltpu.VMEM((rows, heads), bf16),
+            pltpu.VMEM((rows, kv), bf16),
+            pltpu.VMEM((128, kv), bf16),
+            pltpu.VMEM((128, kv), f32),
+            pltpu.VMEM((nc, 16, kv), f32),
+            pltpu.VMEM((rows, kv), f32),
+            pltpu.VMEM((rows, xcols), f32),
+            pltpu.VMEM((ne, rows, cols), bf16),
+            pltpu.VMEM((nt, ne, xcols // ne, heads + kv), bf16),
+            pltpu.VMEM((nt, own, length, heads), bf16),
+            pltpu.VMEM((nt, rows, kv), bf16),
+            pltpu.VMEM((ne, own, length, heads), bf16),
+            pltpu.VMEM((ne, rows, kv), bf16),
+            dma((nc,)),
+            dma((nc,)),
+            dma((nc,)),
+            dma((nc,)),
+            dma((ne,)),
+            dma((ne,)),
+            dma((nt,)),
+            dma((nt,)),
+            dma((ne // 2, nt)),
+            dma((ne, nt)),
+            dma((ne // 2, nt)),
+            dma((own + 1, 2)),
+            dma((own + 1, nt)),
+            dma((own + 1, nt, 2)),
+            dma((own + 1, ne // 2)),
+            dma((own + 1, ne)),
+            dma((own + 1, ne // 2)),
+        ],
+        compiler_params=pltpu.CompilerParams(
+            collective_id=0, has_side_effects=True, vmem_limit_bytes=58 * 2**20
+        ),
+        cost_estimate=pl.CostEstimate(
+            flops=flops, bytes_accessed=16 * 2**20, transcendentals=rows * length * GQ
+        ),
+    )(
+        tokens.reshape(rows, width),
+        qkv_weight.reshape(width, heads + kv),
+        lengths.reshape(own),
+        grad_out.reshape(rows, heads),
+    )
+    return (
+        attended.reshape(1, own, length, 1, heads),
+        grad_x.reshape(1, own, length, xcols),
+        grad_w.reshape(cols, 1, heads + kv),
+    )
+
+
+def local(sizes, tokens, qkv_weight, lengths, grad_out):
+    nc, nt, nd = sizes
+    lists, own, length, width = tokens.shape
+    ne = nc * nd
+    fits = (
+        lists == 1
+        and qkv_weight.shape[1] == 1
+        and nd % 2 == 0
+        and nc * 16 <= 128
+        and own <= 8
+        and width % (ne * 128) == 0
+        and width % (ne * nt * 128) == 0
+        and length % 128 == 0
+        and 2 * ne * own * length * (width // ne) <= 6 * 2**20
+    )
+    if fits:
+        return fused((nc, nt, nd, own, length), tokens, qkv_weight, lengths, grad_out)
+    return body(tokens, qkv_weight, lengths, grad_out)
+
+
 def solution(mesh):
     placed = (
         P("dp", "cand", None, None),
@@ -116,8 +615,9 @@
         P("dp", "cand"),
         P("dp", "cand", None, "tp", None),
     )
+    sizes = tuple(mesh.shape[name] for name in ("cand", "tp", "dp"))
     return jax.shard_map(
-        body,
+        functools.partial(local, sizes),
         mesh=mesh,
         in_specs=placed,
         out_specs=(

time: 341 us -> 170 us (0.50)
  waiting for transfers between devices: 229 us -> 0 us
  Pallas kernels: 0 us -> 162 us
  matrix products: 47.1 us -> 0 us
  other arithmetic: 16.4 us -> 0 us
  blocking collectives: 14.5 us -> 0 us
  between operations: 15 us -> 0.65 us
  local copies, waits for them, and re-layouts: 18.3 us -> 7.1 us
    reduce_scatter x2 -> x0, waiting for transfers between devices: 229 us -> none  [the longest x1 135 us: body(): lax.psum_scatter(partial_x, 'tp', scatter_dimension=1, tiled=True)]
    pallas_call x0 -> x1, Pallas kernels: none -> 162 us  [fused(): pl.pallas_call(functools.partial(kernel, sizes), out_shape=(jax.ShapeDtyp...]
    dot_general x18 -> x0, matrix products: 47.1 us -> none  [the longest x3 11.5 us: attend(): jnp.einsum('chglm,cmhe->clhge', weights, value_rows, precision=highest)]
    all_gather x2 -> x0, blocking collectives: 9.55 us -> none  [the longest x1 5.13 us: body(): lax.all_gather(key_part[:, :, 0], 'cand', axis=1, tiled=True)]
    another operation x6 -> x0, other arithmetic: 8.3 us -> none
    reduce_sum x4 -> x0, other arithmetic: 4.99 us -> none  [the longest x1 4.53 us: attend(): totals = jnp.sum(weights, axis=-1)]
    unnamed x1 -> x0, blocking collectives: 4.94 us -> none
    another operation x9 -> x0, local copies, waits for them, and re-layouts: 3.75 us -> none
  transfers between devices with their start and end apart: 2 -> 0, of which waited for: 2 -> 0; matrix products, arithmetic and copies ran while one was open for 4% -> 0% of each run, Pallas kernels for 0% -> 0%
where the time goes in v1:
time: 170 us
  Pallas kernels  162 us (95%)
  local copies, waits for them, and re-layouts  7.1 us (4%)
    pallas_call x1, Pallas kernels, fused(): pl.pallas_call(functools.partial(kernel, sizes), out_shape=(jax.ShapeDtyp...  162 us
    unnamed x5, local copies, waits for them, and re-layouts  7.1 us

profile of v1, /device:TPU:0, one launch (start us, length us, event | category | flops | bytes accessed | tf_op | source)
XLA Modules:
  0.0 170.0 jit_solution(5836646386397330152)
XLA Ops:
  0.6 162.3 %shard_map.67 = (bf16[512,512]{1,0:T(8,128)(2,1)}, bf16[512,1024]{1,0:T(8,128)(2,1)}, f32[512,768]{1,0:T(8,128)}) custom-call(bf16[512,4096]{1,0:T(8,128)(2,1)} %bitcast.13, bf16[4096,768]{1,0:T(8,128)(2,1)} %bitcast.12, s32[2]{0:T(128)} %bitcast.15, bf16[512,512]{1,0:T(8,128)(2,1)} %bitcast.14), custom_call_target="tpu_custom_call" | custom-call | flops 9663676416 | bytes 16777216 | tf_op jit(solution)/shard_map/pallas_call | solution.py:531
  162.9 0.0 copy-start
  162.9 4.3 %copy.8 = f32[512,1,768]{2,1,0:T(1,128)} copy(f32[512,1,768]{2,0,1:T(8,128)} %bitcast.9) | data formatting | bytes 3145728
  167.2 1.9 %copy.11 = bf16[1,2,256,1,512]{4,2,3,1,0:T(8,128)(2,1)} copy(bf16[1,2,256,1,512]{4,2,3,1,0:T(8,128)(2,1)} %bitcast.11) | data formatting | bytes 1048576
  169.1 0.0 copy-done
  169.1 1.0 copy.12
Async XLA Ops:
  162.9 6.1 %copy-start = (bf16[512,1024]{1,0:T(8,128)(2,1)S(1)}, bf16[512,1024]{1,0:T(8,128)(2,1)}, u32[]{:S(2)}) copy-start(bf16[512,1024]{1,0:T(8,128)(2,1)} %get-tuple-element.7) | copy-start | bytes 3145732

commit v2 on v1

--- a/solution.py
+++ b/solution.py
@@ -152,6 +152,10 @@
     dkvz,
     dqp,
     dkvp,
+    gsq,
+    gsk,
+    grq,
+    grk,
     cls_s,
     cls_r,
     dcls_s,
@@ -169,41 +173,47 @@
     p_s,
     p_r,
     pf_s,
+    g_s,
+    g_r,
 ):
     nc, nt, nd, own, length = sizes
-    ne = nc * nd
+    ny, nx = nd // 2, nc * 2
     c, t, d = lax.axis_index("cand"), lax.axis_index("tp"), lax.axis_index("dp")
-    e = c * nd + d
-    sib = d + 1 - 2 * lax.rem(d, 2)
-    cols = tok.shape[1] // ne
+    y, core = d // 2, lax.rem(d, 2)
+    sib = d + 1 - 2 * core
+    me = c * 2 + core
+    cols = tok.shape[1] // (nc * nd)
     xcols = w.shape[0] // nt
-    part = xcols // ne
-    rows = own * length
+    part = xcols // nd
+    heads = GQ * HD
     scale = 1.0 / math.sqrt(HD)
 
     cls[...] = jnp.zeros_like(cls)
     dcls[...] = jnp.zeros_like(dcls)
     dkv_acc[...] = jnp.zeros_like(dkv_acc)
 
-    def plane(k):
-        j = lax.rem(e + k, ne)
-        return j, {"cand": j // nd, "dp": lax.rem(j, nd)}
-
-    nh = nd // 2
-
-    def chip(k):
-        j = lax.rem(c * nh + d // 2 + k, nc * nh)
-        jc, jd = j // nh, 2 * lax.rem(j, nh) + lax.rem(d, 2)
-        return jc * nd + jd, {"cand": jc, "dp": jd}
+    def row(k):
+        j = lax.rem(me + k, nx)
+        return j, {"cand": j // 2, "dp": 2 * y + lax.rem(j, 2)}
+
+    def along(k):
+        j = lax.rem(c + k, nc)
+        return j * 2 + core, {"cand": j}
+
+    def across(k):
+        j = 2 * lax.rem(y + k, ny) + core
+        return j, {"dp": j}
 
     barrier = pltpu.get_barrier_semaphore()
-    for k in range(1, ne):
-        pl.semaphore_signal(barrier, inc=1, device_id=plane(k)[1], device_id_type=MESH)
+    for k in range(1, nx):
+        pl.semaphore_signal(barrier, inc=1, device_id=row(k)[1], device_id_type=MESH)
+    for k in range(1, ny):
+        pl.semaphore_signal(barrier, inc=1, device_id=across(k)[1], device_id_type=MESH)
     for k in range(1, nt):
         pl.semaphore_signal(
             barrier, inc=1, device_id={"tp": lax.rem(t + k, nt)}, device_id_type=MESH
         )
-    pl.semaphore_wait(barrier, ne - 1 + nt - 1)
+    pl.semaphore_wait(barrier, nx - 1 + ny - 1 + nt - 1)
 
     def remote(src, dst, ss, rs, dev):
         return pltpu.make_async_remote_copy(
@@ -213,8 +223,8 @@
     def wz_send(k):
         o = lax.rem(t + k, nt)
         return remote(
-            w.at[pl.ds(pl.multiple_of(o * xcols + e * part, 16), part)],
-            wg.at[t, e],
+            w.at[pl.ds(pl.multiple_of(o * xcols + d * part, 16), part)],
+            wg.at[t, d],
             wz_s.at[k],
             wz_r.at[t],
             {"tp": o},
@@ -222,10 +232,10 @@
 
     def wz_recv(k):
         h = lax.rem(t + k, nt)
-        return remote(wg.at[h, e], wg.at[h, e], wz_s.at[k], wz_r.at[h], {"tp": h})
+        return remote(wg.at[h, d], wg.at[h, d], wz_s.at[k], wz_r.at[h], {"tp": h})
 
     def wp_send(k, h):
-        return remote(wg.at[h, e], wg.at[h, e], wp_s.at[k, h], wp_r.at[e, h], chip(k)[1])
+        return remote(wg.at[h, d], wg.at[h, d], wp_s.at[k, h], wp_r.at[d, h], across(k)[1])
 
     def wp_sib(j, k, h):
         return remote(wg.at[h, j], wg.at[h, j], wf_s.at[k, h], wp_r.at[j, h], {"dp": sib})
@@ -233,20 +243,32 @@
     def w_wait(j, h):
         remote(wg.at[h, j], wg.at[h, j], wf_s.at[0, h], wp_r.at[j, h], {"dp": sib}).wait_recv()
 
-    def tok_send(k):
-        j, dev = plane(k)
+    def block(cc, step, kk):
+        j = cc * nd + 2 * lax.rem(y + step, ny) + kk
+        return pl.ds(pl.multiple_of(j * cols, 128), cols)
+
+    def tok_send(step, k):
+        j, dev = row(k)
         return remote(
-            tok.at[:, pl.ds(pl.multiple_of(j * cols, 128), cols)],
-            tokg.at[e],
-            tok_s.at[k],
-            tok_r.at[e],
+            tok.at[:, block(j // 2, step, lax.rem(j, 2))],
+            tokg.at[step, me],
+            tok_s.at[step, k],
+            tok_r.at[step, me],
             dev,
         )
 
+    def tok_wait(step):
+        for k in range(1, nx):
+            j, dev = row(k)
+            remote(
+                tokg.at[step, j], tokg.at[step, j], tok_s.at[step, k], tok_r.at[step, j], dev
+            ).wait_recv()
+
     for k in range(1, nt):
         wz_send(k).start()
-    for k in range(1, ne):
-        tok_send(k).start()
+    for step in range(1, ny):
+        for k in range(1, nx):
+            tok_send(step, k).start()
 
     def zbuf(n, s):
         return dqz.at[s, n] if n < own else dkvz.at[s]
@@ -258,10 +280,10 @@
         return remote(zbuf(n, s), zbuf(n, s), ss, z_r.at[n, s], {"tp": to})
 
     def p_send(n, k):
-        return remote(zbuf(n, t), pbuf(n, e), p_s.at[n, k], p_r.at[n, e], chip(k)[1])
+        return remote(zbuf(n, t), pbuf(n, me), p_s.at[n, k], p_r.at[n, me], along(k)[1])
 
     def p_sib(n):
-        return remote(zbuf(n, t), pbuf(n, e), pf_s.at[n, 0], p_r.at[n, e], {"dp": sib})
+        return remote(zbuf(n, t), pbuf(n, me), pf_s.at[n, 0], p_r.at[n, me], {"dp": sib})
 
     def p_fwd(n, j, k):
         return remote(pbuf(n, j), pbuf(n, j), pf_s.at[n, k], p_r.at[n, j], {"dp": sib})
@@ -277,33 +299,39 @@
             def _():
                 z_copy(n, t, to, z_s.at[n, side]).start()
 
-        for k in range(1, nc * nh):
+        for k in range(1, nc):
             p_send(n, k).start()
         p_sib(n).start()
 
-    kvb[...] = dot(tok[...], w[:, GQ * HD :], 1, 0).astype(bf16)
+    kvb[...] = dot(tok[...], w[:, heads:], 1, 0).astype(bf16)
     first = lax.broadcasted_iota(jnp.int32, (16, 2 * HD), 0)
     mine = jnp.zeros((16, 2 * HD), f32)
     for p in range(own):
-        row = kvb[p * length : p * length + 16, :].astype(f32)[0:1]
-        mine = jnp.where(first == p, row, mine)
-    c16 = pl.ds(pl.multiple_of(c * 16, 16), 16)
-    cls[c16, :] = mine.astype(bf16)
+        cls_row = kvb[p * length : p * length + 16, :].astype(f32)[0:1]
+        mine = jnp.where(first == p, cls_row, mine)
+
+    def rows_of(j):
+        return pl.ds(pl.multiple_of(j * 16, 16), 16)
+
+    cls[rows_of(c), :] = mine.astype(bf16)
 
     def cls_send(k):
         return remote(
-            cls.at[c16], cls.at[c16], cls_s.at[k], cls_r.at[c], {"cand": lax.rem(c + k, nc)}
+            cls.at[rows_of(c)], cls.at[rows_of(c)], cls_s.at[k], cls_r.at[c], along(k)[1]
         )
 
     def cls_recv(k):
         o = lax.rem(c + k, nc)
-        o16 = pl.ds(pl.multiple_of(o * 16, 16), 16)
-        return remote(cls.at[o16], cls.at[o16], cls_s.at[k], cls_r.at[o], {"cand": o})
+        return remote(cls.at[rows_of(o)], cls.at[rows_of(o)], cls_s.at[k], cls_r.at[o], {"cand": o})
+
+    def dcls_send(k):
+        o = lax.rem(c + k, nc)
+        return remote(dcls.at[rows_of(o)], dclsr.at[c], dcls_s.at[k], dcls_r.at[c], {"cand": o})
 
     for k in range(1, nc):
         cls_send(k).start()
 
-    @pl.loop(0, GQ * HD // 256)
+    @pl.loop(0, heads // 256)
     def _(i):
         at = pl.ds(pl.multiple_of(i * 256, 256), 256)
         qb[:, at] = dot(tok[...], w[:, at], 1, 0).astype(bf16)
@@ -354,24 +382,11 @@
             dcls[:, HD:] += dot2(pfs, do16, 0, 0)
 
         if p == own - 1:
-            def dcls_send(k):
-                o = lax.rem(c + k, nc)
-                o16 = pl.ds(pl.multiple_of(o * 16, 16), 16)
-                return remote(dcls.at[o16], dclsr.at[c], dcls_s.at[k], dcls_r.at[c], {"cand": o})
-
             for k in range(1, nc):
                 dcls_send(k).start()
         send_chunk(p)
-        if p == 0:
-            for k in range(1, nt):
-                wz_recv(k).wait_recv()
-            for k in range(1, nt):
-                h = lax.rem(t + k, nt)
-                for j in range(1, nc * nh):
-                    wp_send(j, h).start()
-                wp_sib(e, 0, h).start()
-
-    mine = dcls[c16, :]
+
+    mine = dcls[rows_of(c), :]
     for k in range(1, nc):
         o = lax.rem(c + k, nc)
         remote(dclsr.at[o], dclsr.at[o], dcls_s.at[k], dcls_r.at[o], {"cand": o}).wait_recv()
@@ -382,123 +397,153 @@
         dkv_acc[at, :] = dkv_acc[at, :] + jnp.where(top == 0, mine[p : p + 1], 0.0)
     dkvz[t] = dkv_acc[...].astype(bf16)
     send_chunk(own)
+    for k in range(1, nx):
+        tok_send(0, k).start()
 
     def x_terms(h, weight, start):
-        @pl.loop(0, xcols // part)
+        @pl.loop(0, nd)
         def _(i):
             wi = weight(i)
             at = pl.ds(pl.multiple_of(i * part, 128), part)
             for p in range(own):
                 rs = slice(p * length, (p + 1) * length)
-                y = dot(dqz[h, p], wi[:, : GQ * HD], 1, 1)
-                y = y + dot(dkvz[h, rs, :], wi[:, GQ * HD :], 1, 1)
+                v = dot(dqz[h, p], wi[:, :heads], 1, 1)
+                v = v + dot(dkvz[h, rs, :], wi[:, heads:], 1, 1)
                 if start:
-                    gx_acc[rs, at] = y
+                    gx_acc[rs, at] = v
                 else:
-                    gx_acc[rs, at] += y
-
-    def w_terms(x, dq, dkv, start):
-        xs = [x[p * length : (p + 1) * length] for p in range(own)]
-        y = dot(xs[0], dq(0), 0, 0)
+                    gx_acc[rs, at] += v
+
+    def q_terms(x, dq):
+        v = dot(x[:length], dq(0), 0, 0)
         for p in range(1, own):
-            y = y + dot(xs[p], dq(p), 0, 0)
-        z = dot(x, dkv, 0, 0)
-        if start:
-            gw[:, : GQ * HD] = y
-            gw[:, GQ * HD :] = z
-        else:
-            gw[:, : GQ * HD] += y
-            gw[:, GQ * HD :] += z
-
-    x_terms(
-        t, lambda i: w[pl.ds(pl.multiple_of(t * xcols + i * part, 16), part), :], True
-    )
-    w_terms(
-        tok[:, pl.ds(pl.multiple_of(e * cols, 128), cols)],
-        lambda p: dqz[t, p],
-        dkvz[t],
-        True,
-    )
+            v = v + dot(x[p * length : (p + 1) * length], dq(p), 0, 0)
+        return v
+
+    def own_cols(step):
+        return tok[:, block(c, step, core)]
+
+    x_terms(t, lambda i: w[pl.ds(pl.multiple_of(t * xcols + i * part, 16), part), :], True)
+    for step in range(1, ny):
+        x = own_cols(step)
+        gsq[step - 1] = q_terms(x, lambda p: dqz[t, p])
+        gsk[step - 1] = dot(x, dkvz[t], 0, 0)
+    x = own_cols(0)
+    gw[:, :heads] = q_terms(x, lambda p: dqz[t, p])
+    gw[:, heads:] = dot(x, dkvz[t], 0, 0)
+
+    def z_pass(n, dist):
+        for side in (0, 1):
+            src, to = t + dist * (2 * side - 1), t - 2 * side + 1
+
+            @pl.when((src >= 0) & (src < nt))
+            def _():
+                z_copy(n, src, t, zf_s.at[n, dist, side]).wait_recv()
+                if dist < nt - 1:
+
+                    @pl.when((to >= 0) & (to < nt))
+                    def _():
+                        z_copy(n, src, to, zf_s.at[n, dist, side]).start()
 
     for n in range(own + 1):
-        for k in range(1, nc * nh):
-            j = chip(k)[0]
+        z_pass(n, 1)
+        for k in range(1, nc):
+            j = along(k)[0]
             p_wait(n, j)
             p_fwd(n, j, k).start()
-        for side in (0, 1):
-            src, to = t + 2 * side - 1, t - 2 * side + 1
-
-            @pl.when((src >= 0) & (src < nt))
-            def _():
-                z_copy(n, src, t, zf_s.at[n, 1, side]).wait_recv()
-
-                @pl.when((to >= 0) & (to < nt))
-                def _():
-                    z_copy(n, src, to, zf_s.at[n, 1, side]).start()
-
-    for k in range(1, nc * nh):
-        j = chip(k)[0]
+    for k in range(1, nt):
+        wz_recv(k).wait_recv()
+        h = lax.rem(t + k, nt)
+        for j in range(1, ny):
+            wp_send(j, h).start()
+        wp_sib(d, 0, h).start()
+
+    def g_send(step, half):
+        dev = across(step)[1]
+        src, dst = (gsk, grk) if half else (gsq, grq)
+        return remote(
+            src.at[step - 1], dst.at[step - 1], g_s.at[step - 1, half], g_r.at[step - 1, half], dev
+        )
+
+    def sib_wait(n):
+        for k in range(nc):
+            p_wait(n, along(k)[0] + 1 - 2 * core)
+
+    for step in range(1, ny):
+        tok_wait(step)
+    for n in range(own):
+        sib_wait(n)
+    for step in range(1, ny):
+
+        @pl.loop(1, nx)
+        def _(k):
+            j = lax.rem(me + k, nx)
+            gsq[step - 1] += q_terms(tokg[step, j], lambda p: dqp[j, p])
+
+        g_send(step, 0).start()
+    sib_wait(own)
+    for step in range(1, ny):
+
+        @pl.loop(1, nx)
+        def _(k):
+            j = lax.rem(me + k, nx)
+            gsk[step - 1] += dot(tokg[step, j], dkvp[j], 0, 0)
+
+        g_send(step, 1).start()
+
+    for dist in range(2, nt - 1):
+        for n in range(own + 1):
+            z_pass(n, dist)
+
+    for k in range(1, ny):
+        j = across(k)[0]
         for i in range(1, nt):
             h = lax.rem(t + i, nt)
             w_wait(j, h)
             wp_sib(j, k, h).start()
 
-    for dist in range(2, nt):
-        for n in range(own + 1):
-            for side in (0, 1):
-                src, to = t + dist * (2 * side - 1), t - 2 * side + 1
-
-                @pl.when((src >= 0) & (src < nt))
-                def _():
-                    z_copy(n, src, t, zf_s.at[n, dist, side]).wait_recv()
-                    if dist < nt - 1:
-
-                        @pl.when((to >= 0) & (to < nt))
-                        def _():
-                            z_copy(n, src, to, zf_s.at[n, dist, side]).start()
-
-    for k in range(nc * nh):
-        j = chip(k)[0]
-        js = j + 1 - 2 * lax.rem(d, 2)
+    tok_wait(0)
+
+    @pl.loop(1, nx)
+    def _(k):
+        j = lax.rem(me + k, nx)
+        gw[:, :heads] += q_terms(tokg[0, j], lambda p: dqp[j, p])
+        gw[:, heads:] += dot(tokg[0, j], dkvp[j], 0, 0)
+
+    for k in range(ny):
+        j = across(k)[0] + 1 - 2 * core
         for i in range(1, nt):
-            w_wait(js, lax.rem(t + i, nt))
+            w_wait(j, lax.rem(t + i, nt))
+    for n in range(own + 1):
+        z_pass(n, nt - 1)
 
     @pl.loop(1, nt)
-    def _(i):
-        h = lax.rem(t + i, nt)
+    def _(k):
+        h = lax.rem(t + k, nt)
         x_terms(h, lambda i: wg[h, i], False)
 
     gx[...] = gx_acc[...].astype(bf16)
 
-    for k in range(nc * nh):
-        j = chip(k)[0]
-        js = j + 1 - 2 * lax.rem(d, 2)
-        for n in range(own + 1):
-            p_wait(n, js)
-    for k in range(1, ne):
-        j = plane(k)[0]
-        remote(tokg.at[j], tokg.at[j], tok_s.at[k], tok_r.at[j], {"dp": sib}).wait_recv()
-
-    @pl.loop(1, ne)
-    def _(k):
-        j = lax.rem(e + k, ne)
-        w_terms(tokg[j], lambda p: dqp[j, p], dkvp[j], False)
+    for step in range(1, ny):
+        g_send(step, 0).wait_recv()
+        gw[:, :heads] += grq[step - 1]
+        g_send(step, 1).wait_recv()
+        gw[:, heads:] += grk[step - 1]
 
     for k in range(1, nt):
         wz_send(k).wait_send()
-    for k in range(1, ne):
-        tok_send(k).wait_send()
+    for step in range(ny):
+        for k in range(1, nx):
+            tok_send(step, k).wait_send()
     for k in range(1, nc):
         cls_send(k).wait_send()
-        o = lax.rem(c + k, nc)
-        o16 = pl.ds(pl.multiple_of(o * 16, 16), 16)
-        remote(dcls.at[o16], dclsr.at[c], dcls_s.at[k], dcls_r.at[c], {"cand": o}).wait_send()
+        dcls_send(k).wait_send()
     for i in range(1, nt):
         h = lax.rem(t + i, nt)
-        for k in range(1, nc * nh):
+        for k in range(1, ny):
             wp_send(k, h).wait_send()
-            wp_sib(chip(k)[0], k, h).wait_send()
-        wp_sib(e, 0, h).wait_send()
+            wp_sib(across(k)[0], k, h).wait_send()
+        wp_sib(d, 0, h).wait_send()
     for n in range(own + 1):
         for side in (0, 1):
             to = t + 2 * side - 1
@@ -514,16 +559,20 @@
                 def _():
                     z_copy(n, src, on, zf_s.at[n, dist, side]).wait_send()
 
-        for k in range(1, nc * nh):
+        for k in range(1, nc):
             p_send(n, k).wait_send()
-            p_fwd(n, chip(k)[0], k).wait_send()
+            p_fwd(n, along(k)[0], k).wait_send()
         p_sib(n).wait_send()
+    for step in range(1, ny):
+        g_send(step, 0).wait_send()
+        g_send(step, 1).wait_send()
 
 
 def fused(sizes, tokens, qkv_weight, lengths, grad_out):
     nc, nt, nd, own, length = sizes
-    ne, width, rows = nc * nd, tokens.shape[-1], own * length
-    cols, xcols = width // ne, width // nt
+    ny, nx = nd // 2, nc * 2
+    width, rows = tokens.shape[-1], own * length
+    cols, xcols = width // (nc * nd), width // nt
     kv, heads = 2 * HD, GQ * HD
     dma = pltpu.SemaphoreType.DMA
     vmem = pl.BlockSpec(memory_space=pltpu.VMEM)
@@ -545,29 +594,35 @@
             pltpu.VMEM((nc, 16, kv), f32),
             pltpu.VMEM((rows, kv), f32),
             pltpu.VMEM((rows, xcols), f32),
-            pltpu.VMEM((ne, rows, cols), bf16),
-            pltpu.VMEM((nt, ne, xcols // ne, heads + kv), bf16),
+            pltpu.VMEM((ny, nx, rows, cols), bf16),
+            pltpu.VMEM((nt, nd, xcols // nd, heads + kv), bf16),
             pltpu.VMEM((nt, own, length, heads), bf16),
             pltpu.VMEM((nt, rows, kv), bf16),
-            pltpu.VMEM((ne, own, length, heads), bf16),
-            pltpu.VMEM((ne, rows, kv), bf16),
+            pltpu.VMEM((nx, own, length, heads), bf16),
+            pltpu.VMEM((nx, rows, kv), bf16),
+            pltpu.VMEM((ny - 1, cols, heads), f32),
+            pltpu.VMEM((ny - 1, cols, kv), f32),
+            pltpu.VMEM((ny - 1, cols, heads), f32),
+            pltpu.VMEM((ny - 1, cols, kv), f32),
             dma((nc,)),
             dma((nc,)),
             dma((nc,)),
             dma((nc,)),
-            dma((ne,)),
-            dma((ne,)),
+            dma((ny, nx)),
+            dma((ny, nx)),
             dma((nt,)),
             dma((nt,)),
-            dma((ne // 2, nt)),
-            dma((ne, nt)),
-            dma((ne // 2, nt)),
+            dma((ny, nt)),
+            dma((nd, nt)),
+            dma((ny, nt)),
             dma((own + 1, 2)),
             dma((own + 1, nt)),
             dma((own + 1, nt, 2)),
-            dma((own + 1, ne // 2)),
-            dma((own + 1, ne)),
-            dma((own + 1, ne // 2)),
+            dma((own + 1, nc)),
+            dma((own + 1, nx)),
+            dma((own + 1, nc)),
+            dma((ny - 1, 2)),
+            dma((ny - 1, 2)),
         ],
         compiler_params=pltpu.CompilerParams(
             collective_id=0, has_side_effects=True, vmem_limit_bytes=58 * 2**20
@@ -596,10 +651,13 @@
         lists == 1
         and qkv_weight.shape[1] == 1
         and nd % 2 == 0
+        and nd >= 4
+        and nc >= 2
+        and nt >= 3
         and nc * 16 <= 128
         and own <= 8
         and width % (ne * 128) == 0
-        and width % (ne * nt * 128) == 0
+        and width % (nd * nt * 128) == 0
         and length % 128 == 0
         and 2 * ne * own * length * (width // ne) <= 6 * 2**20
     )

time: 170 us -> 131 us (0.77)
  the two profiles are of different devices: /device:TPU:0 before, /device:TPU:8 now
where the time goes in v2:
time: 131 us; the launch traced here: 130 us
  Pallas kernels  123 us (94%)
  local copies, waits for them, and re-layouts  7.1 us (5%)
    pallas_call x1, Pallas kernels, fused(): pl.pallas_call(functools.partial(kernel, sizes), out_shape=(jax.ShapeDtyp...  123 us
    unnamed x5, local copies, waits for them, and re-layouts  7.1 us

profile of v2, /device:TPU:8, one launch (start us, length us, event | category | flops | bytes accessed | tf_op | source)
XLA Modules:
  0.0 130.3 jit_solution(8686877383367878622)
XLA Ops:
  0.6 122.6 %shard_map.67 = (bf16[512,512]{1,0:T(8,128)(2,1)}, bf16[512,1024]{1,0:T(8,128)(2,1)}, f32[512,768]{1,0:T(8,128)}) custom-call(bf16[512,4096]{1,0:T(8,128)(2,1)} %bitcast.13, bf16[4096,768]{1,0:T(8,128)(2,1)} %bitcast.12, s32[2]{0:T(128)} %bitcast.15, bf16[512,512]{1,0:T(8,128)(2,1)} %bitcast.14), custom_call_target="tpu_custom_call" | custom-call | flops 9663676416 | bytes 16777216 | tf_op jit(solution)/shard_map/pallas_call | solution.py:580
  123.2 0.0 copy-start
  123.3 4.3 %copy.8 = f32[512,1,768]{2,1,0:T(1,128)} copy(f32[512,1,768]{2,0,1:T(8,128)} %bitcast.9) | data formatting | bytes 3145728
  127.5 1.9 %copy.11 = bf16[1,2,256,1,512]{4,2,3,1,0:T(8,128)(2,1)} copy(bf16[1,2,256,1,512]{4,2,3,1,0:T(8,128)(2,1)} %bitcast.11) | data formatting | bytes 1048576
  129.4 0.0 copy-done
  129.4 1.0 copy.12
Async XLA Ops:
  123.2 6.1 %copy-start = (bf16[512,1024]{1,0:T(8,128)(2,1)S(1)}, bf16[512,1024]{1,0:T(8,128)(2,1)}, u32[]{:S(2)}) copy-start(bf16[512,1024]{1,0:T(8,128)(2,1)} %get-tuple-element.7) | copy-start | bytes 3145732

commit v3 on v2

--- a/solution.py
+++ b/solution.py
@@ -145,6 +145,7 @@
     dcls,
     dclsr,
     dkv_acc,
+    turned,
     gx_acc,
     tokg,
     wg,
@@ -190,7 +191,6 @@
 
     cls[...] = jnp.zeros_like(cls)
     dcls[...] = jnp.zeros_like(dcls)
-    dkv_acc[...] = jnp.zeros_like(dkv_acc)
 
     def row(k):
         j = lax.rem(me + k, nx)
@@ -349,38 +349,43 @@
         listed = (far_row == 0) & (lax.rem(far_lane, 16) < own) & (far_lane < nc * 16)
         listed = listed & (far_lane != c * 16 + p)
 
-        @pl.loop(0, GQ)
+        turned[...] = jnp.zeros_like(turned)
+
+        @pl.loop(0, GQ, unroll=2)
         def _(g):
             head = pl.ds(pl.multiple_of(g * HD, HD), HD)
             q, do = qb[at, head], go[at, head]
             k, v = kvb[at, :HD], kvb[at, HD:]
             ck, cv = cls[:, :HD], cls[:, HD:]
             q16, do16 = q[:16], do[:16]
-            s = jnp.where(visible, dot(q, k, 1, 1) * scale, masked_value)
-            f = jnp.where(listed, dot(q16, ck, 1, 1) * scale, masked_value)
+            s = jnp.where(visible, dot(q, k, 1, 1), masked_value)
+            f = jnp.where(listed, dot(q16, ck, 1, 1), masked_value)
             m = jnp.max(s, axis=1, keepdims=True)
             m16 = jnp.maximum(m[:16], jnp.max(f, axis=1, keepdims=True))
             m = jnp.concatenate([m16, m[16:]], axis=0)
-            pr, pf = jnp.exp(s - m), jnp.exp(f - m16)
+            pr, pf = jnp.exp((s - m) * scale), jnp.exp((f - m16) * scale)
             total = jnp.sum(pr, axis=1, keepdims=True)
             t16 = total[:16] + jnp.sum(pf, axis=1, keepdims=True)
             total = jnp.concatenate([t16, total[16:]], axis=0)
-            pr, pf = pr / total, pf / t16
+            over = 1.0 / total
+            pr, pf = pr * over, pf * over[:16]
             prs, pfs = split(pr), split(pf)
             o = dot2(prs, v, 1, 0)
             o = jnp.concatenate([o[:16] + dot2(pfs, cv, 1, 0), o[16:]], axis=0)
             att[at, head] = o.astype(bf16)
             delta = jnp.sum(o * do.astype(f32), axis=1, keepdims=True)
-            ds = split(pr * (dot(do, v, 1, 1) - delta) * scale)
+            ds = split(pr * (dot(do, v, 1, 1) - delta))
             dsf = split(pf * (dot(do16, cv, 1, 1) - delta[:16]) * scale)
-            dq = dot2(ds, k, 1, 0)
+            dq = dot2(ds, k, 1, 0) * scale
             dq = jnp.concatenate([dq[:16] + dot2(dsf, ck, 1, 0), dq[16:]], axis=0)
             dqz[t, p, :, head] = dq.astype(bf16)
-            dkv_acc[at, :HD] += dot2(ds, q, 0, 0)
-            dkv_acc[at, HD:] += dot2(prs, do, 0, 0)
+            turned[:HD, :] += dot(q, ds[0], 0, 0) + dot(q, ds[1], 0, 0)
+            turned[HD:, :] += dot(do, prs[0], 0, 0) + dot(do, prs[1], 0, 0)
             dcls[:, :HD] += dot2(dsf, q16, 0, 0)
             dcls[:, HD:] += dot2(pfs, do16, 0, 0)
 
+        dkv_acc[at, :HD] = turned[:HD, :].T * scale
+        dkv_acc[at, HD:] = turned[HD:, :].T
         if p == own - 1:
             for k in range(1, nc):
                 dcls_send(k).start()
@@ -424,6 +429,13 @@
         return tok[:, block(c, step, core)]
 
     x_terms(t, lambda i: w[pl.ds(pl.multiple_of(t * xcols + i * part, 16), part), :], True)
+    for k in range(1, nt):
+        wz_recv(k).wait_recv()
+        h = lax.rem(t + k, nt)
+        for j in range(1, ny):
+            wp_send(j, h).start()
+        wp_sib(d, 0, h).start()
+
     for step in range(1, ny):
         x = own_cols(step)
         gsq[step - 1] = q_terms(x, lambda p: dqz[t, p])
@@ -451,13 +463,6 @@
             j = along(k)[0]
             p_wait(n, j)
             p_fwd(n, j, k).start()
-    for k in range(1, nt):
-        wz_recv(k).wait_recv()
-        h = lax.rem(t + k, nt)
-        for j in range(1, ny):
-            wp_send(j, h).start()
-        wp_sib(d, 0, h).start()
-
     def g_send(step, half):
         dev = across(step)[1]
         src, dst = (gsk, grk) if half else (gsq, grq)
@@ -514,13 +519,16 @@
         j = across(k)[0] + 1 - 2 * core
         for i in range(1, nt):
             w_wait(j, lax.rem(t + i, nt))
-    for n in range(own + 1):
-        z_pass(n, nt - 1)
-
-    @pl.loop(1, nt)
-    def _(k):
-        h = lax.rem(t + k, nt)
-        x_terms(h, lambda i: wg[h, i], False)
+    for dist in range(1, nt):
+        if dist == nt - 1:
+            for n in range(own + 1):
+                z_pass(n, dist)
+        for side in (0, 1):
+            src = t + dist * (2 * side - 1)
+
+            @pl.when((src >= 0) & (src < nt))
+            def _():
+                x_terms(src, lambda i: wg[src, i], False)
 
     gx[...] = gx_acc[...].astype(bf16)
 
@@ -593,6 +601,7 @@
             pltpu.VMEM((128, kv), f32),
             pltpu.VMEM((nc, 16, kv), f32),
             pltpu.VMEM((rows, kv), f32),
+            pltpu.VMEM((kv, length), f32),
             pltpu.VMEM((rows, xcols), f32),
             pltpu.VMEM((ny, nx, rows, cols), bf16),
             pltpu.VMEM((nt, nd, xcols // nd, heads + kv), bf16),

time: 131 us -> 118 us (0.901)
  the two profiles are of different devices: /device:TPU:8 before, /device:TPU:0 now
where the time goes in v3:
time: 118 us
  Pallas kernels  110 us (93%)
  local copies, waits for them, and re-layouts  7.1 us (6%)
    pallas_call x1, Pallas kernels, fused(): pl.pallas_call(functools.partial(kernel, sizes), out_shape=(jax.ShapeDtyp...  110 us
    unnamed x5, local copies, waits for them, and re-layouts  7.1 us

profile of v3, /device:TPU:0, one launch (start us, length us, event | category | flops | bytes accessed | tf_op | source)
XLA Modules:
  0.0 117.7 jit_solution(765277916317643547)
XLA Ops:
  0.6 109.9 %shard_map.67 = (bf16[512,512]{1,0:T(8,128)(2,1)}, bf16[512,1024]{1,0:T(8,128)(2,1)}, f32[512,768]{1,0:T(8,128)}) custom-call(bf16[512,4096]{1,0:T(8,128)(2,1)} %bitcast.13, bf16[4096,768]{1,0:T(8,128)(2,1)} %bitcast.12, s32[2]{0:T(128)} %bitcast.15, bf16[512,512]{1,0:T(8,128)(2,1)} %bitcast.14), custom_call_target="tpu_custom_call" | custom-call | flops 9663676416 | bytes 16777216 | tf_op jit(solution)/shard_map/pallas_call | solution.py:588
  110.6 0.0 copy-start
  110.6 4.3 %copy.8 = f32[512,1,768]{2,1,0:T(1,128)} copy(f32[512,1,768]{2,0,1:T(8,128)} %bitcast.9) | data formatting | bytes 3145728
  114.8 1.9 %copy.11 = bf16[1,2,256,1,512]{4,2,3,1,0:T(8,128)(2,1)} copy(bf16[1,2,256,1,512]{4,2,3,1,0:T(8,128)(2,1)} %bitcast.11) | data formatting | bytes 1048576
  116.7 0.0 copy-done
  116.7 1.0 copy.12
Async XLA Ops:
  110.6 6.1 %copy-start = (bf16[512,1024]{1,0:T(8,128)(2,1)S(1)}, bf16[512,1024]{1,0:T(8,128)(2,1)}, u32[]{:S(2)}) copy-start(bf16[512,1024]{1,0:T(8,128)(2,1)} %get-tuple-element.7) | copy-start | bytes 3145732

commit v4 on v3

--- a/solution.py
+++ b/solution.py
@@ -157,6 +157,7 @@
     gsk,
     grq,
     grk,
+    gw_acc,
     cls_s,
     cls_r,
     dcls_s,
@@ -167,53 +168,56 @@
     wz_r,
     wp_s,
     wp_r,
-    wf_s,
     z_s,
     z_r,
     zf_s,
     p_s,
     p_r,
-    pf_s,
     g_s,
     g_r,
 ):
     nc, nt, nd, own, length = sizes
-    ny, nx = nd // 2, nc * 2
     c, t, d = lax.axis_index("cand"), lax.axis_index("tp"), lax.axis_index("dp")
     y, core = d // 2, lax.rem(d, 2)
-    sib = d + 1 - 2 * core
-    me = c * 2 + core
     cols = tok.shape[1] // (nc * nd)
     xcols = w.shape[0] // nt
-    part = xcols // nd
+    part = xcols // (nc * nd)
     heads = GQ * HD
     scale = 1.0 / math.sqrt(HD)
 
     cls[...] = jnp.zeros_like(cls)
     dcls[...] = jnp.zeros_like(dcls)
 
-    def row(k):
-        j = lax.rem(me + k, nx)
-        return j, {"cand": j // 2, "dp": 2 * y + lax.rem(j, 2)}
-
-    def along(k):
-        j = lax.rem(c + k, nc)
-        return j * 2 + core, {"cand": j}
-
-    def across(k):
-        j = 2 * lax.rem(y + k, ny) + core
-        return j, {"dp": j}
+    def at_x(kk):
+        return {"cand": 1 - c, "dp": 2 * y + kk}
+
+    def at_y(kk):
+        return {"cand": c, "dp": 2 * (1 - y) + kk}
+
+    def index(dev):
+        return dev["cand"] * nd + dev["dp"]
+
+    flip = 1 - core
+    sib = {"cand": c, "dp": 2 * y + flip}
+    gather = {"cand": c * core + (1 - c) * flip, "dp": 2 * (y * flip + (1 - y) * core) + core}
+    add = {"cand": c * flip + (1 - c) * core, "dp": 2 * (y * core + (1 - y) * flip) + core}
+    e, e_sib, e_gather, e_add = c * nd + d, index(sib), index(gather), index(add)
+    e_far = (1 - c) * nd + 2 * (1 - y) + core
+    sib_add = (c * core + (1 - c) * flip) * nd + 2 * (y * flip + (1 - y) * core) + flip
+    users = (
+        (sib, 0, (e_sib, sib_add)),
+        (at_x(0), 1 + core, (index(at_x(0)), (1 - c) * nd + 2 * (1 - y))),
+        (at_y(1), 1 + core, (index(at_y(1)), (1 - c) * nd + 2 * (1 - y) + 1)),
+    )
 
     barrier = pltpu.get_barrier_semaphore()
-    for k in range(1, nx):
-        pl.semaphore_signal(barrier, inc=1, device_id=row(k)[1], device_id_type=MESH)
-    for k in range(1, ny):
-        pl.semaphore_signal(barrier, inc=1, device_id=across(k)[1], device_id_type=MESH)
+    for dev in (sib, at_x(0), at_x(1), at_y(0), at_y(1)):
+        pl.semaphore_signal(barrier, inc=1, device_id=dev, device_id_type=MESH)
     for k in range(1, nt):
         pl.semaphore_signal(
             barrier, inc=1, device_id={"tp": lax.rem(t + k, nt)}, device_id_type=MESH
         )
-    pl.semaphore_wait(barrier, nx - 1 + ny - 1 + nt - 1)
+    pl.semaphore_wait(barrier, 5 + nt - 1)
 
     def remote(src, dst, ss, rs, dev):
         return pltpu.make_async_remote_copy(
@@ -223,8 +227,8 @@
     def wz_send(k):
         o = lax.rem(t + k, nt)
         return remote(
-            w.at[pl.ds(pl.multiple_of(o * xcols + d * part, 16), part)],
-            wg.at[t, d],
+            w.at[pl.ds(pl.multiple_of(o * xcols + e * part, 16), part)],
+            wg.at[t, e],
             wz_s.at[k],
             wz_r.at[t],
             {"tp": o},
@@ -232,42 +236,48 @@
 
     def wz_recv(k):
         h = lax.rem(t + k, nt)
-        return remote(wg.at[h, d], wg.at[h, d], wz_s.at[k], wz_r.at[h], {"tp": h})
-
-    def wp_send(k, h):
-        return remote(wg.at[h, d], wg.at[h, d], wp_s.at[k, h], wp_r.at[d, h], across(k)[1])
-
-    def wp_sib(j, k, h):
-        return remote(wg.at[h, j], wg.at[h, j], wf_s.at[k, h], wp_r.at[j, h], {"dp": sib})
-
-    def w_wait(j, h):
-        remote(wg.at[h, j], wg.at[h, j], wf_s.at[0, h], wp_r.at[j, h], {"dp": sib}).wait_recv()
-
-    def block(cc, step, kk):
-        j = cc * nd + 2 * lax.rem(y + step, ny) + kk
+        return remote(wg.at[h, e], wg.at[h, e], wz_s.at[k], wz_r.at[h], {"tp": h})
+
+    def wp(k, j, h, dev):
+        return remote(wg.at[h, j], wg.at[h, j], wp_s.at[k, h], wp_r.at[j, h], dev)
+
+    w_first = ((0, e, at_x(core)), (1, e, at_y(core)), (2, e, sib))
+    w_second = ((3, e_gather, add), (4, e_gather, sib), (5, e_add, sib))
+    w_third = ((6, e_far, sib),)
+
+    def w_start(copies):
+        for i in range(1, nt):
+            for k, j, dev in copies:
+                wp(k, j, lax.rem(t + i, nt), dev).start()
+
+    def w_wait(slots):
+        for i in range(1, nt):
+            for j in slots:
+                wp(0, j, lax.rem(t + i, nt), sib).wait_recv()
+
+    def block(j):
         return pl.ds(pl.multiple_of(j * cols, 128), cols)
 
     def tok_send(step, k):
-        j, dev = row(k)
+        dev, slot, blocks = users[k]
         return remote(
-            tok.at[:, block(j // 2, step, lax.rem(j, 2))],
-            tokg.at[step, me],
+            tok.at[:, block(blocks[step])],
+            tokg.at[step, slot],
             tok_s.at[step, k],
-            tok_r.at[step, me],
+            tok_r.at[step, slot],
             dev,
         )
 
     def tok_wait(step):
-        for k in range(1, nx):
-            j, dev = row(k)
+        for k in range(3):
             remote(
-                tokg.at[step, j], tokg.at[step, j], tok_s.at[step, k], tok_r.at[step, j], dev
+                tokg.at[step, k], tokg.at[step, k], tok_s.at[step, k], tok_r.at[step, k], sib
             ).wait_recv()
 
     for k in range(1, nt):
         wz_send(k).start()
-    for step in range(1, ny):
-        for k in range(1, nx):
+    for step in (1, 0):
+        for k in range(3):
             tok_send(step, k).start()
 
     def zbuf(n, s):
@@ -280,16 +290,12 @@
         return remote(zbuf(n, s), zbuf(n, s), ss, z_r.at[n, s], {"tp": to})
 
     def p_send(n, k):
-        return remote(zbuf(n, t), pbuf(n, me), p_s.at[n, k], p_r.at[n, me], along(k)[1])
-
-    def p_sib(n):
-        return remote(zbuf(n, t), pbuf(n, me), pf_s.at[n, 0], p_r.at[n, me], {"dp": sib})
-
-    def p_fwd(n, j, k):
-        return remote(pbuf(n, j), pbuf(n, j), pf_s.at[n, k], p_r.at[n, j], {"dp": sib})
-
-    def p_wait(n, j):
-        remote(pbuf(n, j), pbuf(n, j), pf_s.at[n, 0], p_r.at[n, j], {"dp": sib}).wait_recv()
+        dev, slot, _ = users[k]
+        return remote(zbuf(n, t), pbuf(n, slot), p_s.at[n, k], p_r.at[n, slot], dev)
+
+    def p_wait(n):
+        for k in range(3):
+            remote(pbuf(n, k), pbuf(n, k), p_s.at[n, k], p_r.at[n, k], sib).wait_recv()
 
     def send_chunk(n):
         for side in (0, 1):
@@ -299,9 +305,8 @@
             def _():
                 z_copy(n, t, to, z_s.at[n, side]).start()
 
-        for k in range(1, nc):
+        for k in range(3):
             p_send(n, k).start()
-        p_sib(n).start()
 
     kvb[...] = dot(tok[...], w[:, heads:], 1, 0).astype(bf16)
     first = lax.broadcasted_iota(jnp.int32, (16, 2 * HD), 0)
@@ -317,7 +322,7 @@
 
     def cls_send(k):
         return remote(
-            cls.at[rows_of(c)], cls.at[rows_of(c)], cls_s.at[k], cls_r.at[c], along(k)[1]
+            cls.at[rows_of(c)], cls.at[rows_of(c)], cls_s.at[k], cls_r.at[c], {"cand": lax.rem(c + k, nc)}
         )
 
     def cls_recv(k):
@@ -390,6 +395,10 @@
             for k in range(1, nc):
                 dcls_send(k).start()
         send_chunk(p)
+        if p == 0:
+            for k in range(1, nt):
+                wz_recv(k).wait_recv()
+            w_start(w_first)
 
     mine = dcls[rows_of(c), :]
     for k in range(1, nc):
@@ -402,14 +411,11 @@
         dkv_acc[at, :] = dkv_acc[at, :] + jnp.where(top == 0, mine[p : p + 1], 0.0)
     dkvz[t] = dkv_acc[...].astype(bf16)
     send_chunk(own)
-    for k in range(1, nx):
-        tok_send(0, k).start()
-
     def x_terms(h, weight, start):
         @pl.loop(0, nd)
         def _(i):
             wi = weight(i)
-            at = pl.ds(pl.multiple_of(i * part, 128), part)
+            at = pl.ds(pl.multiple_of(i * nc * part, 128), nc * part)
             for p in range(own):
                 rs = slice(p * length, (p + 1) * length)
                 v = dot(dqz[h, p], wi[:, :heads], 1, 1)
@@ -425,24 +431,14 @@
             v = v + dot(x[p * length : (p + 1) * length], dq(p), 0, 0)
         return v
 
-    def own_cols(step):
-        return tok[:, block(c, step, core)]
-
-    x_terms(t, lambda i: w[pl.ds(pl.multiple_of(t * xcols + i * part, 16), part), :], True)
-    for k in range(1, nt):
-        wz_recv(k).wait_recv()
-        h = lax.rem(t + k, nt)
-        for j in range(1, ny):
-            wp_send(j, h).start()
-        wp_sib(d, 0, h).start()
-
-    for step in range(1, ny):
-        x = own_cols(step)
-        gsq[step - 1] = q_terms(x, lambda p: dqz[t, p])
-        gsk[step - 1] = dot(x, dkvz[t], 0, 0)
-    x = own_cols(0)
-    gw[:, :heads] = q_terms(x, lambda p: dqz[t, p])
-    gw[:, heads:] = dot(x, dkvz[t], 0, 0)
+    wide = nc * part
+    x_terms(t, lambda i: w[pl.ds(pl.multiple_of(t * xcols + i * wide, 16), wide), :], True)
+    x = tok[:, block(e_add)]
+    gsq[...] = q_terms(x, lambda p: dqz[t, p])
+    gsk[...] = dot(x, dkvz[t], 0, 0)
+    x = tok[:, block(e)]
+    gw_acc[:, :heads] = q_terms(x, lambda p: dqz[t, p])
+    gw_acc[:, heads:] = dot(x, dkvz[t], 0, 0)
 
     def z_pass(n, dist):
         for side in (0, 1):
@@ -459,66 +455,43 @@
 
     for n in range(own + 1):
         z_pass(n, 1)
-        for k in range(1, nc):
-            j = along(k)[0]
-            p_wait(n, j)
-            p_fwd(n, j, k).start()
-    def g_send(step, half):
-        dev = across(step)[1]
+    w_wait((e_gather, e_add))
+    w_start(w_second)
+
+    def g_send(half):
         src, dst = (gsk, grk) if half else (gsq, grq)
-        return remote(
-            src.at[step - 1], dst.at[step - 1], g_s.at[step - 1, half], g_r.at[step - 1, half], dev
-        )
-
-    def sib_wait(n):
-        for k in range(nc):
-            p_wait(n, along(k)[0] + 1 - 2 * core)
-
-    for step in range(1, ny):
-        tok_wait(step)
+        return remote(src, dst, g_s.at[half], g_r.at[half], add)
+
+    tok_wait(1)
     for n in range(own):
-        sib_wait(n)
-    for step in range(1, ny):
-
-        @pl.loop(1, nx)
-        def _(k):
-            j = lax.rem(me + k, nx)
-            gsq[step - 1] += q_terms(tokg[step, j], lambda p: dqp[j, p])
-
-        g_send(step, 0).start()
-    sib_wait(own)
-    for step in range(1, ny):
-
-        @pl.loop(1, nx)
-        def _(k):
-            j = lax.rem(me + k, nx)
-            gsk[step - 1] += dot(tokg[step, j], dkvp[j], 0, 0)
-
-        g_send(step, 1).start()
+        p_wait(n)
+
+    @pl.loop(0, 3)
+    def _(k):
+        gsq[...] += q_terms(tokg[1, k], lambda p: dqp[k, p])
+
+    g_send(0).start()
+    p_wait(own)
+
+    @pl.loop(0, 3)
+    def _(k):
+        gsk[...] += dot(tokg[1, k], dkvp[k], 0, 0)
+
+    g_send(1).start()
 
     for dist in range(2, nt - 1):
         for n in range(own + 1):
             z_pass(n, dist)
-
-    for k in range(1, ny):
-        j = across(k)[0]
-        for i in range(1, nt):
-            h = lax.rem(t + i, nt)
-            w_wait(j, h)
-            wp_sib(j, k, h).start()
-
+    w_wait((e_far,))
+    w_start(w_third)
     tok_wait(0)
 
-    @pl.loop(1, nx)
+    @pl.loop(0, 3)
     def _(k):
-        j = lax.rem(me + k, nx)
-        gw[:, :heads] += q_terms(tokg[0, j], lambda p: dqp[j, p])
-        gw[:, heads:] += dot(tokg[0, j], dkvp[j], 0, 0)
-
-    for k in range(ny):
-        j = across(k)[0] + 1 - 2 * core
-        for i in range(1, nt):
-            w_wait(j, lax.rem(t + i, nt))
+        gw_acc[:, :heads] += q_terms(tokg[0, k], lambda p: dqp[k, p])
+        gw_acc[:, heads:] += dot(tokg[0, k], dkvp[k], 0, 0)
+
+    w_wait([j * nd + 2 * i + flip for j in range(nc) for i in range(nd // 2)])
     for dist in range(1, nt):
         if dist == nt - 1:
             for n in range(own + 1):
@@ -528,30 +501,36 @@
 
             @pl.when((src >= 0) & (src < nt))
             def _():
-                x_terms(src, lambda i: wg[src, i], False)
+                x_terms(
+                    src,
+                    lambda i: wg[src, pl.ds(i * nc, nc)].reshape(wide, heads + 2 * HD),
+                    False,
+                )
 
     gx[...] = gx_acc[...].astype(bf16)
 
-    for step in range(1, ny):
-        g_send(step, 0).wait_recv()
-        gw[:, :heads] += grq[step - 1]
-        g_send(step, 1).wait_recv()
-        gw[:, heads:] += grk[step - 1]
+    g_send(0).wait_recv()
+    g_send(1).wait_recv()
+    chunks = (heads + 2 * HD) // 128
+    for i in range(chunks):
+        if i * 128 < heads:
+            v = grq[:, i * 128 : (i + 1) * 128]
+        else:
+            v = grk[:, i * 128 - heads : (i + 1) * 128 - heads]
+        gw[pl.ds(i, cols, stride=chunks), :] = v + gw_acc[:, i * 128 : (i + 1) * 128]
 
     for k in range(1, nt):
         wz_send(k).wait_send()
-    for step in range(ny):
-        for k in range(1, nx):
+    for step in (0, 1):
+        for k in range(3):
             tok_send(step, k).wait_send()
     for k in range(1, nc):
         cls_send(k).wait_send()
         dcls_send(k).wait_send()
     for i in range(1, nt):
         h = lax.rem(t + i, nt)
-        for k in range(1, ny):
-            wp_send(k, h).wait_send()
-            wp_sib(across(k)[0], k, h).wait_send()
-        wp_sib(d, 0, h).wait_send()
+        for k, j, dev in w_first + w_second + w_third:
+            wp(k, j, h, dev).wait_send()
     for n in range(own + 1):
         for side in (0, 1):
             to = t + 2 * side - 1
@@ -567,18 +546,14 @@
                 def _():
                     z_copy(n, src, on, zf_s.at[n, dist, side]).wait_send()
 
-        for k in range(1, nc):
+        for k in range(3):
             p_send(n, k).wait_send()
-            p_fwd(n, along(k)[0], k).wait_send()
-        p_sib(n).wait_send()
-    for step in range(1, ny):
-        g_send(step, 0).wait_send()
-        g_send(step, 1).wait_send()
+    g_send(0).wait_send()
+    g_send(1).wait_send()
 
 
 def fused(sizes, tokens, qkv_weight, lengths, grad_out):
     nc, nt, nd, own, length = sizes
-    ny, nx = nd // 2, nc * 2
     width, rows = tokens.shape[-1], own * length
     cols, xcols = width // (nc * nd), width // nt
     kv, heads = 2 * HD, GQ * HD
@@ -590,7 +565,7 @@
         out_shape=(
             jax.ShapeDtypeStruct((rows, heads), bf16),
             jax.ShapeDtypeStruct((rows, xcols), bf16),
-            jax.ShapeDtypeStruct((cols, heads + kv), f32),
+            jax.ShapeDtypeStruct((cols * (heads + kv) // 128, 128), f32),
         ),
         in_specs=[vmem, vmem, pl.BlockSpec(memory_space=pltpu.SMEM), vmem],
         out_specs=(vmem, vmem, vmem),
@@ -603,35 +578,34 @@
             pltpu.VMEM((rows, kv), f32),
             pltpu.VMEM((kv, length), f32),
             pltpu.VMEM((rows, xcols), f32),
-            pltpu.VMEM((ny, nx, rows, cols), bf16),
-            pltpu.VMEM((nt, nd, xcols // nd, heads + kv), bf16),
+            pltpu.VMEM((2, 3, rows, cols), bf16),
+            pltpu.VMEM((nt, nc * nd, xcols // (nc * nd), heads + kv), bf16),
             pltpu.VMEM((nt, own, length, heads), bf16),
             pltpu.VMEM((nt, rows, kv), bf16),
-            pltpu.VMEM((nx, own, length, heads), bf16),
-            pltpu.VMEM((nx, rows, kv), bf16),
-            pltpu.VMEM((ny - 1, cols, heads), f32),
-            pltpu.VMEM((ny - 1, cols, kv), f32),
-            pltpu.VMEM((ny - 1, cols, heads), f32),
-            pltpu.VMEM((ny - 1, cols, kv), f32),
+            pltpu.VMEM((3, own, length, heads), bf16),
+            pltpu.VMEM((3, rows, kv), bf16),
+            pltpu.VMEM((cols, heads), f32),
+            pltpu.VMEM((cols, kv), f32),
+            pltpu.VMEM((cols, heads), f32),
+            pltpu.VMEM((cols, kv), f32),
+            pltpu.VMEM((cols, heads + kv), f32),
             dma((nc,)),
             dma((nc,)),
             dma((nc,)),
             dma((nc,)),
-            dma((ny, nx)),
-            dma((ny, nx)),
+            dma((2, 3)),
+            dma((2, 3)),
             dma((nt,)),
             dma((nt,)),
-            dma((ny, nt)),
-            dma((nd, nt)),
-            dma((ny, nt)),
+            dma((7, nt)),
+            dma((nc * nd, nt)),
             dma((own + 1, 2)),
             dma((own + 1, nt)),
             dma((own + 1, nt, 2)),
-            dma((own + 1, nc)),
-            dma((own + 1, nx)),
-            dma((own + 1, nc)),
-            dma((ny - 1, 2)),
-            dma((ny - 1, 2)),
+            dma((own + 1, 3)),
+            dma((own + 1, 3)),
+            dma((2,)),
+            dma((2,)),
         ],
         compiler_params=pltpu.CompilerParams(
             collective_id=0, has_side_effects=True, vmem_limit_bytes=58 * 2**20
@@ -659,14 +633,12 @@
     fits = (
         lists == 1
         and qkv_weight.shape[1] == 1
-        and nd % 2 == 0
-        and nd >= 4
-        and nc >= 2
+        and nd == 4
+        and nc == 2
         and nt >= 3
-        and nc * 16 <= 128
         and own <= 8
         and width % (ne * 128) == 0
-        and width % (nd * nt * 128) == 0
+        and width % (ne * nt * 128) == 0
         and length % 128 == 0
         and 2 * ne * own * length * (width // ne) <= 6 * 2**20
     )

time: 118 us -> 108 us (0.915)
  Pallas kernels: 110 us -> 101 us
  local copies, waits for them, and re-layouts: 7.1 us -> 5.39 us
    pallas_call x1, Pallas kernels: 110 us -> 101 us  [fused(): pl.pallas_call(functools.partial(kernel, sizes), out_shape=(jax.ShapeDtyp...]
    unnamed x5, local copies, waits for them, and re-layouts: 7.1 us -> 5.39 us
where the time goes in v4:
time: 108 us
  Pallas kernels  101 us (94%)
  local copies, waits for them, and re-layouts  5.39 us (5%)
    pallas_call x1, Pallas kernels, fused(): pl.pallas_call(functools.partial(kernel, sizes), out_shape=(jax.ShapeDtyp...  101 us
    unnamed x5, local copies, waits for them, and re-layouts  5.39 us

profile of v4, /device:TPU:0, one launch (start us, length us, event | category | flops | bytes accessed | tf_op | source)
XLA Modules:
  0.0 107.5 jit_solution(12587858928826393832)
XLA Ops:
  0.6 101.5 %shard_map.67 = (bf16[512,512]{1,0:T(8,128)(2,1)}, bf16[512,1024]{1,0:T(8,128)(2,1)}, f32[3072,128]{1,0:T(8,128)}) custom-call(bf16[512,4096]{1,0:T(8,128)(2,1)} %bitcast.13, bf16[4096,768]{1,0:T(8,128)(2,1)} %bitcast.12, s32[2]{0:T(128)} %bitcast.15, bf16[512,512]{1,0:T(8,128)(2,1)} %bitcast.14), custom_call_target="tpu_custom_call" | custom-call | flops 9663676416 | bytes 16777216 | tf_op jit(solution)/shard_map/pallas_call | solution.py:563
  102.1 0.0 copy-start
  102.1 2.0 %copy.12 = bf16[1,2,256,1,512]{4,2,3,1,0:T(8,128)(2,1)} copy(bf16[1,2,256,1,512]{4,2,3,1,0:T(8,128)(2,1)} %bitcast.11) | data formatting | bytes 1048576
  104.1 2.3 %copy.13 = bf16[1,2,256,1024]{3,2,1,0:T(8,128)(2,1)} copy(bf16[1,2,256,1024]{3,2,1,0:T(8,128)(2,1)} %bitcast.10) | data formatting | bytes 2097152
  106.4 0.0 copy-done
  106.4 1.1 %copy.14 = f32[512,1,768]{2,1,0:T(1,128)} copy(f32[512,1,768]{2,1,0:T(1,128)S(1)} %bitcast.9) | data formatting | bytes 3145728
Async XLA Ops:
  102.1 4.3 %copy-start = (f32[3072,128]{1,0:T(8,128)S(1)}, f32[3072,128]{1,0:T(8,128)}, u32[]{:S(2)}) copy-start(f32[3072,128]{1,0:T(8,128)} %get-tuple-element.8) | copy-start | bytes 4718596

commit v5 on v4

--- a/solution.py
+++ b/solution.py
@@ -132,13 +132,17 @@
 
 def kernel(
     sizes,
-    tok,
-    w,
+    tok_h,
+    w_h,
     lens,
-    go,
+    go_h,
     att,
     gx,
     gw,
+    tok,
+    w,
+    go,
+    ld,
     qb,
     kvb,
     cls,
@@ -185,6 +189,21 @@
     heads = GQ * HD
     scale = 1.0 / math.sqrt(HD)
 
+    kv_cols, q_cols = pl.ds(heads, 2 * HD), pl.ds(0, heads)
+    loads = [
+        pltpu.make_async_copy(a, b, ld.at[i])
+        for i, (a, b) in enumerate(
+            (
+                (w_h.at[:, kv_cols], w.at[:, kv_cols]),
+                (tok_h, tok),
+                (w_h.at[:, q_cols], w.at[:, q_cols]),
+                (go_h, go),
+            )
+        )
+    ]
+    for load in loads:
+        load.start()
+
     cls[...] = jnp.zeros_like(cls)
     dcls[...] = jnp.zeros_like(dcls)
 
@@ -227,7 +246,7 @@
     def wz_send(k):
         o = lax.rem(t + k, nt)
         return remote(
-            w.at[pl.ds(pl.multiple_of(o * xcols + e * part, 16), part)],
+            w_h.at[pl.ds(pl.multiple_of(o * xcols + e * part, 16), part)],
             wg.at[t, e],
             wz_s.at[k],
             wz_r.at[t],
@@ -261,7 +280,7 @@
     def tok_send(step, k):
         dev, slot, blocks = users[k]
         return remote(
-            tok.at[:, block(blocks[step])],
+            tok_h.at[:, block(blocks[step])],
             tokg.at[step, slot],
             tok_s.at[step, k],
             tok_r.at[step, slot],
@@ -308,6 +327,21 @@
         for k in range(3):
             p_send(n, k).start()
 
+    def z_pass(n, dist):
+        for side in (0, 1):
+            src, to = t + dist * (2 * side - 1), t - 2 * side + 1
+
+            @pl.when((src >= 0) & (src < nt))
+            def _():
+                z_copy(n, src, t, zf_s.at[n, dist, side]).wait_recv()
+                if dist < nt - 1:
+
+                    @pl.when((to >= 0) & (to < nt))
+                    def _():
+                        z_copy(n, src, to, zf_s.at[n, dist, side]).start()
+
+    loads[0].wait()
+    loads[1].wait()
     kvb[...] = dot(tok[...], w[:, heads:], 1, 0).astype(bf16)
     first = lax.broadcasted_iota(jnp.int32, (16, 2 * HD), 0)
     mine = jnp.zeros((16, 2 * HD), f32)
@@ -336,6 +370,8 @@
     for k in range(1, nc):
         cls_send(k).start()
 
+    loads[2].wait()
+
     @pl.loop(0, heads // 256)
     def _(i):
         at = pl.ds(pl.multiple_of(i * 256, 256), 256)
@@ -344,6 +380,7 @@
     for k in range(1, nc):
         cls_recv(k).wait_recv()
 
+    loads[3].wait()
     far_lane = lax.broadcasted_iota(jnp.int32, (16, 128), 1)
     far_row = lax.broadcasted_iota(jnp.int32, (16, 128), 0)
     lane = lax.broadcasted_iota(jnp.int32, (length, length), 1)
@@ -399,6 +436,8 @@
             for k in range(1, nt):
                 wz_recv(k).wait_recv()
             w_start(w_first)
+        if p > 0:
+            z_pass(p - 1, 1)
 
     mine = dcls[rows_of(c), :]
     for k in range(1, nc):
@@ -433,6 +472,7 @@
 
     wide = nc * part
     x_terms(t, lambda i: w[pl.ds(pl.multiple_of(t * xcols + i * wide, 16), wide), :], True)
+    z_pass(own - 1, 1)
     x = tok[:, block(e_add)]
     gsq[...] = q_terms(x, lambda p: dqz[t, p])
     gsk[...] = dot(x, dkvz[t], 0, 0)
@@ -440,21 +480,10 @@
     gw_acc[:, :heads] = q_terms(x, lambda p: dqz[t, p])
     gw_acc[:, heads:] = dot(x, dkvz[t], 0, 0)
 
-    def z_pass(n, dist):
-        for side in (0, 1):
-            src, to = t + dist * (2 * side - 1), t - 2 * side + 1
-
-            @pl.when((src >= 0) & (src < nt))
-            def _():
-                z_copy(n, src, t, zf_s.at[n, dist, side]).wait_recv()
-                if dist < nt - 1:
-
-                    @pl.when((to >= 0) & (to < nt))
-                    def _():
-                        z_copy(n, src, to, zf_s.at[n, dist, side]).start()
-
-    for n in range(own + 1):
-        z_pass(n, 1)
+    z_pass(own, 1)
+    for dist in range(2, nt - 1):
+        for n in range(own):
+            z_pass(n, dist)
     w_wait((e_gather, e_add))
     w_start(w_second)
 
@@ -471,6 +500,8 @@
         gsq[...] += q_terms(tokg[1, k], lambda p: dqp[k, p])
 
     g_send(0).start()
+    for dist in range(2, nt - 1):
+        z_pass(own, dist)
     p_wait(own)
 
     @pl.loop(0, 3)
@@ -479,9 +510,6 @@
 
     g_send(1).start()
 
-    for dist in range(2, nt - 1):
-        for n in range(own + 1):
-            z_pass(n, dist)
     w_wait((e_far,))
     w_start(w_third)
     tok_wait(0)
@@ -552,13 +580,29 @@
     g_send(1).wait_send()
 
 
+PIECES = 4
+
+
+def publish(a, b, c, a_out, b_out, c_out, sem):
+    copies = []
+    for i, (src, dst) in enumerate(((a, a_out), (b, b_out), (c, c_out))):
+        rows = src.shape[0] // PIECES
+        for j in range(PIECES):
+            at = pl.ds(j * rows, rows)
+            copies.append(pltpu.make_async_copy(src.at[at], dst.at[at], sem.at[i, j]))
+    for copy in copies:
+        copy.start()
+    for copy in copies:
+        copy.wait()
+
+
 def fused(sizes, tokens, qkv_weight, lengths, grad_out):
     nc, nt, nd, own, length = sizes
     width, rows = tokens.shape[-1], own * length
     cols, xcols = width // (nc * nd), width // nt
     kv, heads = 2 * HD, GQ * HD
     dma = pltpu.SemaphoreType.DMA
-    vmem = pl.BlockSpec(memory_space=pltpu.VMEM)
+    vmem, hbm = pl.BlockSpec(memory_space=pltpu.VMEM), pl.BlockSpec(memory_space=pl.ANY)
     flops = 6 * rows * width * (heads + kv)
     attended, grad_x, grad_w = pl.pallas_call(
         functools.partial(kernel, sizes),
@@ -567,9 +611,13 @@
             jax.ShapeDtypeStruct((rows, xcols), bf16),
             jax.ShapeDtypeStruct((cols * (heads + kv) // 128, 128), f32),
         ),
-        in_specs=[vmem, vmem, pl.BlockSpec(memory_space=pltpu.SMEM), vmem],
+        in_specs=[hbm, hbm, pl.BlockSpec(memory_space=pltpu.SMEM), hbm],
         out_specs=(vmem, vmem, vmem),
         scratch_shapes=[
+            pltpu.VMEM((rows, width), bf16),
+            pltpu.VMEM((width, heads + kv), bf16),
+            pltpu.VMEM((rows, heads), bf16),
+            dma((4,)),
             pltpu.VMEM((rows, heads), bf16),
             pltpu.VMEM((rows, kv), bf16),
             pltpu.VMEM((128, kv), bf16),
@@ -619,6 +667,15 @@
         lengths.reshape(own),
         grad_out.reshape(rows, heads),
     )
+    results = (attended, grad_x, grad_w)
+    attended, grad_x, grad_w = pl.pallas_call(
+        publish,
+        out_shape=tuple(jax.ShapeDtypeStruct(a.shape, a.dtype) for a in results),
+        in_specs=[hbm] * 3,
+        out_specs=(hbm,) * 3,
+        scratch_shapes=[dma((3, PIECES))],
+        compiler_params=pltpu.CompilerParams(vmem_limit_bytes=62 * 2**20),
+    )(*results)
     return (
         attended.reshape(1, own, length, 1, heads),
         grad_x.reshape(1, own, length, xcols),

time: 108 us -> 196 us (1.81)
  Pallas kernels: 101 us -> 195 us
  local copies, waits for them, and re-layouts: 5.39 us -> 0 us
    pallas_call x0 -> x1, Pallas kernels: none -> 96.5 us  [fused(): pl.pallas_call(publish, out_shape=tuple((jax.ShapeDtypeStruct(a.shape, a....]
    unnamed x5 -> x0, local copies, waits for them, and re-layouts: 5.39 us -> none
    pallas_call x1, Pallas kernels: 101 us -> 99 us  [fused(): pl.pallas_call(functools.partial(kernel, sizes), out_shape=(jax.ShapeDtyp...]
where the time goes in v5:
time: 196 us
  Pallas kernels  195 us (99%)
    pallas_call x1, Pallas kernels, fused(): pl.pallas_call(functools.partial(kernel, sizes), out_shape=(jax.ShapeDtyp...  99 us
    pallas_call x1, Pallas kernels, fused(): pl.pallas_call(publish, out_shape=tuple((jax.ShapeDtypeStruct(a.shape, a....  96.5 us

profile of v5, /device:TPU:0, one launch (start us, length us, event | category | flops | bytes accessed | tf_op | source)
XLA Modules:
  0.0 196.1 jit_solution(3778673221622175360)
XLA Ops:
  0.6 99.0 %shard_map.67 = (bf16[512,512]{1,0:T(8,128)(2,1)}, bf16[512,1024]{1,0:T(8,128)(2,1)}, f32[3072,128]{1,0:T(8,128)}) custom-call(bf16[512,4096]{1,0:T(8,128)(2,1)} %bitcast.10, bf16[4096,768]{1,0:T(8,128)(2,1)} %bitcast.9, s32[2]{0:T(128)} %bitcast.15, bf16[512,512]{1,0:T(8,128)(2,1)} %bitcast.13), custom_call_target="tpu_custom_call" | custom-call | flops 9663676416 | bytes 16777216 | tf_op jit(solution)/shard_map/pallas_call | solution.py:607
  99.6 96.5 %shard_map.68 = (bf16[512,512]{1,0:T(8,128)(2,1)}, bf16[512,1024]{1,0:T(8,128)(2,1)}, f32[3072,128]{1,0:T(8,128)}) custom-call(bf16[512,512]{1,0:T(8,128)(2,1)} %get-tuple-element.9.a, bf16[512,1024]{1,0:T(8,128)(2,1)} %get-tuple-element.10.b, f32[3072,128]{1,0:T(8,128)} %get-tuple-element.11.c), custom_call_target="tpu_custom_call" | custom-call | tf_op jit(solution)/shard_map/pallas_call | solution.py:671

commit v6 on v5

--- a/solution.py
+++ b/solution.py
@@ -371,15 +371,6 @@
         cls_send(k).start()
 
     loads[2].wait()
-
-    @pl.loop(0, heads // 256)
-    def _(i):
-        at = pl.ds(pl.multiple_of(i * 256, 256), 256)
-        qb[:, at] = dot(tok[...], w[:, at], 1, 0).astype(bf16)
-
-    for k in range(1, nc):
-        cls_recv(k).wait_recv()
-
     loads[3].wait()
     far_lane = lax.broadcasted_iota(jnp.int32, (16, 128), 1)
     far_row = lax.broadcasted_iota(jnp.int32, (16, 128), 0)
@@ -393,8 +384,16 @@
 
         turned[...] = jnp.zeros_like(turned)
 
-        @pl.loop(0, GQ, unroll=2)
-        def _(g):
+        @pl.loop(0, heads // 256)
+        def _(i):
+            to = pl.ds(pl.multiple_of(i * 256, 256), 256)
+            qb[at, to] = dot(tok[at, :], w[:, to], 1, 0).astype(bf16)
+
+        if p == 0:
+            for k in range(1, nc):
+                cls_recv(k).wait_recv()
+
+        def one_head(g):
             head = pl.ds(pl.multiple_of(g * HD, HD), HD)
             q, do = qb[at, head], go[at, head]
             k, v = kvb[at, :HD], kvb[at, HD:]
@@ -426,16 +425,20 @@
             dcls[:, :HD] += dot2(dsf, q16, 0, 0)
             dcls[:, HD:] += dot2(pfs, do16, 0, 0)
 
+        if p < own - 1:
+            pl.loop(0, GQ, unroll=2)(one_head)
+        else:
+            pl.loop(0, GQ // 2, unroll=2)(one_head)
+            for k in range(1, nt):
+                wz_recv(k).wait_recv()
+            w_start(w_first)
+            pl.loop(GQ // 2, GQ, unroll=2)(one_head)
         dkv_acc[at, :HD] = turned[:HD, :].T * scale
         dkv_acc[at, HD:] = turned[HD:, :].T
         if p == own - 1:
             for k in range(1, nc):
                 dcls_send(k).start()
         send_chunk(p)
-        if p == 0:
-            for k in range(1, nt):
-                wz_recv(k).wait_recv()
-            w_start(w_first)
         if p > 0:
             z_pass(p - 1, 1)
 
@@ -583,17 +586,27 @@
 PIECES = 4
 
 
-def publish(a, b, c, a_out, b_out, c_out, sem):
-    copies = []
-    for i, (src, dst) in enumerate(((a, a_out), (b, b_out), (c, c_out))):
+def publish(a, b, c, a_out, b_out, c_out, a_mid, b_mid, c_mid, sem_in, sem_out):
+    moves = []
+    for i, (src, mid, dst) in enumerate(
+        ((a, a_mid, a_out), (b, b_mid, b_out), (c, c_mid, c_out))
+    ):
         rows = src.shape[0] // PIECES
         for j in range(PIECES):
             at = pl.ds(j * rows, rows)
-            copies.append(pltpu.make_async_copy(src.at[at], dst.at[at], sem.at[i, j]))
-    for copy in copies:
-        copy.start()
-    for copy in copies:
-        copy.wait()
+            moves.append(
+                (
+                    pltpu.make_async_copy(src.at[at], mid.at[at], sem_in.at[i, j]),
+                    pltpu.make_async_copy(mid.at[at], dst.at[at], sem_out.at[i, j]),
+                )
+            )
+    for load, _ in moves:
+        load.start()
+    for load, store in moves:
+        load.wait()
+        store.start()
+    for _, store in moves:
+        store.wait()
 
 
 def fused(sizes, tokens, qkv_weight, lengths, grad_out):
@@ -673,7 +686,8 @@
         out_shape=tuple(jax.ShapeDtypeStruct(a.shape, a.dtype) for a in results),
         in_specs=[hbm] * 3,
         out_specs=(hbm,) * 3,
-        scratch_shapes=[dma((3, PIECES))],
+        scratch_shapes=[pltpu.VMEM(a.shape, a.dtype) for a in results]
+        + [dma((3, PIECES)), dma((3, PIECES))],
         compiler_params=pltpu.CompilerParams(vmem_limit_bytes=62 * 2**20),
     )(*results)
     return (

time: 196 us -> 103 us (0.53)
  Pallas kernels: 195 us -> 102 us
    pallas_call x1, Pallas kernels: 96.5 us -> 3.07 us  [fused(): pl.pallas_call(publish, out_shape=tuple((jax.ShapeDtypeStruct(a.shape, a....]
where the time goes in v6:
time: 103 us
  Pallas kernels  102 us (99%)
    pallas_call x1, Pallas kernels, fused(): pl.pallas_call(functools.partial(kernel, sizes), out_shape=(jax.ShapeDtyp...  98.9 us
    pallas_call x1, Pallas kernels, fused(): pl.pallas_call(publish, out_shape=tuple((jax.ShapeDtypeStruct(a.shape, a....  3.07 us

profile of v6, /device:TPU:0, one launch (start us, length us, event | category | flops | bytes accessed | tf_op | source)
XLA Modules:
  0.0 102.7 jit_solution(1298200952572686771)
XLA Ops:
  0.6 98.9 %shard_map.67 = (bf16[512,512]{1,0:T(8,128)(2,1)}, bf16[512,1024]{1,0:T(8,128)(2,1)}, f32[3072,128]{1,0:T(8,128)}) custom-call(bf16[512,4096]{1,0:T(8,128)(2,1)} %bitcast.10, bf16[4096,768]{1,0:T(8,128)(2,1)} %bitcast.9, s32[2]{0:T(128)} %bitcast.15, bf16[512,512]{1,0:T(8,128)(2,1)} %bitcast.13), custom_call_target="tpu_custom_call" | custom-call | flops 9663676416 | bytes 16777216 | tf_op jit(solution)/shard_map/pallas_call | solution.py:620
  99.6 3.1 %shard_map.68 = (bf16[512,512]{1,0:T(8,128)(2,1)}, bf16[512,1024]{1,0:T(8,128)(2,1)}, f32[3072,128]{1,0:T(8,128)}) custom-call(bf16[512,512]{1,0:T(8,128)(2,1)} %get-tuple-element.9.a, bf16[512,1024]{1,0:T(8,128)(2,1)} %get-tuple-element.10.b, f32[3072,128]{1,0:T(8,128)} %get-tuple-element.11.c), custom_call_target="tpu_custom_call" | custom-call | tf_op jit(solution)/shard_map/pallas_call | solution.py:684

commit v7 on v6

--- a/solution.py
+++ b/solution.py
@@ -487,8 +487,6 @@
     for dist in range(2, nt - 1):
         for n in range(own):
             z_pass(n, dist)
-    w_wait((e_gather, e_add))
-    w_start(w_second)
 
     def g_send(half):
         src, dst = (gsk, grk) if half else (gsq, grq)
@@ -503,6 +501,8 @@
         gsq[...] += q_terms(tokg[1, k], lambda p: dqp[k, p])
 
     g_send(0).start()
+    w_wait((e_gather, e_add))
+    w_start(w_second)
     for dist in range(2, nt - 1):
         z_pass(own, dist)
     p_wait(own)

time: 103 us -> 105 us (1.019)
  Pallas kernels: 102 us -> 105 us
    pallas_call x1, Pallas kernels: 98.9 us -> 102 us  [fused(): pl.pallas_call(functools.partial(kernel, sizes), out_shape=(jax.ShapeDtyp...]
where the time goes in v7:
time: 105 us
  Pallas kernels  105 us (100%)
    pallas_call x1, Pallas kernels, fused(): pl.pallas_call(functools.partial(kernel, sizes), out_shape=(jax.ShapeDtyp...  102 us
    pallas_call x1, Pallas kernels, fused(): pl.pallas_call(publish, out_shape=tuple((jax.ShapeDtypeStruct(a.shape, a....  3.07 us

profile of v7, /device:TPU:0, one launch (start us, length us, event | category | flops | bytes accessed | tf_op | source)
XLA Modules:
  0.0 105.3 jit_solution(15023118224332160213)
XLA Ops:
  0.6 101.6 %shard_map.67 = (bf16[512,512]{1,0:T(8,128)(2,1)}, bf16[512,1024]{1,0:T(8,128)(2,1)}, f32[3072,128]{1,0:T(8,128)}) custom-call(bf16[512,4096]{1,0:T(8,128)(2,1)} %bitcast.10, bf16[4096,768]{1,0:T(8,128)(2,1)} %bitcast.9, s32[2]{0:T(128)} %bitcast.15, bf16[512,512]{1,0:T(8,128)(2,1)} %bitcast.13), custom_call_target="tpu_custom_call" | custom-call | flops 9663676416 | bytes 16777216 | tf_op jit(solution)/shard_map/pallas_call | solution.py:620
  102.2 3.1 %shard_map.68 = (bf16[512,512]{1,0:T(8,128)(2,1)}, bf16[512,1024]{1,0:T(8,128)(2,1)}, f32[3072,128]{1,0:T(8,128)}) custom-call(bf16[512,512]{1,0:T(8,128)(2,1)} %get-tuple-element.9.a, bf16[512,1024]{1,0:T(8,128)(2,1)} %get-tuple-element.10.b, f32[3072,128]{1,0:T(8,128)} %get-tuple-element.11.c), custom_call_target="tpu_custom_call" | custom-call | tf_op jit(solution)/shard_map/pallas_call | solution.py:684
